TPU v7x, 32 devices: a whole 2x2x4 slice. The times are simulated.
32 devices in a mesh: req: 4 (over z), wide: 8 (over y, x, core).
Axes of the slice: x: 2, y: 2, z: 4, core: 2. Of those that a mesh axis runs over, the one named last changes fastest.
Arguments:
- queries: bfloat16 [4096, 3072], P(('req', 'wide'))
- suffix_latent: bfloat16 [4096, 512], P(('req', 'wide')), may hold values from -6 to 6
- suffix_rope: bfloat16 [64, 4096], P(None, ('req', 'wide')), may hold values from -6 to 6
- residual: bfloat16 [4096, 2048], P(('req', 'wide')), may hold values from -3 to 3
- prefix_latent: bfloat16 [4, 2, 1024, 512], P('req', None, 'wide'), may hold values from -6 to 6
- prefix_rope: bfloat16 [4, 2, 64, 1024], P('req', None, None, 'wide')
- suffix_lengths: int32 [32, 4], P(('req', 'wide')), may hold values from 1 to 64, 128 in all within a row
- prefix_ids: int32 [32, 4], P(('req', 'wide')), may hold values from 0 to 1
- w_ukv: bfloat16 [512, 4096], replicated, may hold values from -0.25 to 0.25
- w_out: bfloat16 [2048, 2048], replicated, may hold values from -0.5 to 0.5
- norm_gain: bfloat16 [2048], replicated, may hold values from 0.099609375 to 1.8984375
- expert_ids: int32 [4096, 6], P(('req', 'wide')), may hold values from 0 to 15, all different within a row; in each aligned block of 128 rows (0 to 127, 128 to 255, ...) at most 49 rows name the same one
- gate_values: float32 [4096, 6], P(('req', 'wide')), may hold values from 0.05 to 0.45
- expert_gate_up: bfloat16 [32, 2048, 1408], P(('req', 'wide')), may hold values from -0.125 to 0.125
- expert_down: bfloat16 [32, 704, 2048], P(('req', 'wide')), may hold values from -0.15625 to 0.15625
Outputs:
- layer_out: bfloat16 [4096, 2048], P(('req', 'wide'))
Inputs may be any that keep to these rules, and one draw needn't show every extreme that they name: `suffix_lengths`: row b gives, in order, the lengths of the 4 requests that make up tokens b * 128 to (b + 1) * 128 - 1; each row sums to 128 and its largest entry is 64. `expert_ids`: a token's 6 experts differ; among the 128 tokens of one device no expert is named more than 49 times, and in some device one expert is named exactly 49 times.
All inputs are finite; a program needn't handle non-finite values.
Results may differ from a plain program's by a relative error of at most 0.012.
Values may be sent and summed in bfloat16 or wider, within the bound.
A program may use at most 192 MiB of HBM per device.

v0:
```python
import jax
import jax.numpy as jnp
from jax import lax
from jax.sharding import PartitionSpec as P

D = 2048
HEADS = 16
NOPE = 128
ROPE = 64
LAT = 512
TOP = 6
PREF = 2


epsilon = 1e-06


def request_tables(lengths, request_ids, token_count):
    request_end = jnp.cumsum(lengths)
    positions = jnp.arange(token_count, dtype=jnp.int32)
    segment = jnp.sum((positions[:, None] >= request_end[None, :]).astype(jnp.int32), axis=1)
    matches = segment[:, None] == jnp.arange(request_ids.shape[0], dtype=jnp.int32)[None, :]
    prefix = jnp.sum(jnp.where(matches, request_ids[None, :], 0), axis=1)
    return (segment, prefix)


def split_kv(latent, w_ukv):
    row_count = latent.shape[0]
    joined = jnp.dot(latent, w_ukv, preferred_element_type=jnp.float32).astype(jnp.bfloat16)
    joined = joined.reshape(row_count, HEADS, 2 * NOPE).transpose(1, 0, 2)
    return (joined[:, :, :NOPE], joined[:, :, NOPE:])


def split_queries(query_rows):
    row_count = query_rows.shape[0]
    query_nope = query_rows[:, : HEADS * NOPE].reshape(row_count, HEADS, NOPE).transpose(1, 0, 2)
    query_rope = query_rows[:, HEADS * NOPE :].reshape(row_count, HEADS, ROPE).transpose(1, 0, 2)
    return (query_nope, query_rope)


def head_scores(head_nope, head_rope, head_keys, rope_keys):
    scaling = 1.0 / (NOPE + ROPE) ** 0.5
    content = lax.dot_general(
        head_nope, head_keys, (((1,), (1,)), ((), ())), preferred_element_type=jnp.float32
    )
    rotary = jnp.dot(head_rope, rope_keys, preferred_element_type=jnp.float32)
    return (content + rotary) * scaling


def block_partials(query_nope, query_rope, block_keys, block_values, rope_keys, allowed):

    def one_head(operands):
        head_nope, head_rope, head_keys, head_values = operands
        scores = jnp.where(
            allowed, head_scores(head_nope, head_rope, head_keys, rope_keys), -jnp.inf
        )
        maximum = jnp.max(scores, axis=1).astype(jnp.bfloat16)
        weights = jnp.where(allowed, jnp.exp(scores - maximum.astype(jnp.float32)[:, None]), 0.0)
        summed = jnp.sum(weights, axis=1).astype(jnp.bfloat16)
        weighted = jnp.dot(
            weights.astype(jnp.bfloat16), head_values, preferred_element_type=jnp.float32
        ).astype(jnp.bfloat16)
        return (weighted, maximum, summed)

    return lax.map(one_head, (query_nope, query_rope, block_keys, block_values))


def body(
    queries,
    suffix_latent,
    suffix_rope,
    residual,
    prefix_latent,
    prefix_rope,
    suffix_lengths,
    prefix_ids,
    w_ukv,
    w_out,
    norm_gain,
    expert_ids,
    gate_values,
    expert_gate_up,
    expert_down,
):
    token_count = queries.shape[0]
    req_count = lax.axis_size("req")
    wide_count = lax.axis_size("wide")
    segment, prefix = request_tables(suffix_lengths[0], prefix_ids[0], token_count)
    query_nope, query_rope = split_queries(queries)
    block_rows = prefix_latent.shape[2]
    key_owner = jnp.repeat(jnp.arange(PREF, dtype=jnp.int32), block_rows)
    group_prefix = lax.all_gather(prefix, "wide", axis=0, tiled=True)
    prefix_keys, prefix_values = split_kv(prefix_latent[0].reshape(PREF * block_rows, LAT), w_ukv)
    rope_keys = prefix_rope[0].transpose(1, 0, 2).reshape(ROPE, PREF * block_rows)
    piece_allowed = group_prefix[:, None] == key_owner[None, :]
    piece_nope, piece_rope = split_queries(lax.all_gather(queries, "wide", axis=0, tiled=True))
    remote_out, remote_max, remote_sum = block_partials(
        piece_nope, piece_rope, prefix_keys, prefix_values, rope_keys, piece_allowed
    )
    remote_out, remote_max, remote_sum = (
        lax.all_to_all(remote_out, "wide", split_axis=1, concat_axis=1, tiled=True),
        lax.all_to_all(remote_max, "wide", split_axis=1, concat_axis=1, tiled=True),
        lax.all_to_all(remote_sum, "wide", split_axis=1, concat_axis=1, tiled=True),
    )
    far_max = remote_max.astype(jnp.float32).reshape(HEADS, wide_count, token_count)
    far_sum = remote_sum.astype(jnp.float32).reshape(HEADS, wide_count, token_count)
    far_out = remote_out.reshape(HEADS, wide_count, token_count, NOPE)
    suffix_keys, suffix_values = split_kv(suffix_latent, w_ukv)
    positions = jnp.arange(token_count, dtype=jnp.int32)
    causal = (segment[:, None] == segment[None, :]) & (positions[None, :] <= positions[:, None])

    def local_head(operands):
        head_nope, head_rope, head_keys, head_values = operands
        scores = jnp.where(
            causal, head_scores(head_nope, head_rope, head_keys, suffix_rope), -jnp.inf
        )
        maximum = jnp.max(scores, axis=1)
        weights = jnp.where(causal, jnp.exp(scores - maximum[:, None]), 0.0)
        weighted = jnp.dot(
            weights.astype(jnp.bfloat16), head_values, preferred_element_type=jnp.float32
        )
        return (weighted, maximum, jnp.sum(weights, axis=1))

    local_out, local_max, local_sum = lax.map(
        local_head, (query_nope, query_rope, suffix_keys, suffix_values)
    )
    largest = jnp.maximum(local_max, jnp.max(far_max, axis=1))
    far_weight = jnp.exp(far_max - largest[:, None, :])
    near_weight = jnp.exp(local_max - largest)
    numerator = near_weight[:, :, None] * local_out + jnp.sum(
        far_weight[:, :, :, None] * far_out.astype(jnp.float32), axis=1
    )
    denominator = near_weight * local_sum + jnp.sum(far_weight * far_sum, axis=1)
    head_out = (numerator / denominator[:, :, None]).astype(jnp.bfloat16)
    attention = jnp.einsum(
        "htn,hnd->td", head_out, w_out.reshape(HEADS, NOPE, D), preferred_element_type=jnp.float32
    )
    hidden = (residual.astype(jnp.float32) + attention).astype(jnp.bfloat16)
    hidden_f32 = hidden.astype(jnp.float32)
    inverse = lax.rsqrt(jnp.mean(hidden_f32 * hidden_f32, axis=1, keepdims=True) + epsilon)
    normed = (hidden_f32 * inverse * norm_gain.astype(jnp.float32)[None, :]).astype(jnp.bfloat16)
    experts = req_count * wide_count // 2
    capacity = token_count * TOP // experts + 1
    flat_ids = expert_ids.reshape(-1)
    one_hot = (flat_ids[:, None] == jnp.arange(experts, dtype=jnp.int32)[None, :]).astype(jnp.int32)
    slot_index = jnp.sum((jnp.cumsum(one_hot, axis=0) - 1) * one_hot, axis=1)
    target = flat_ids * capacity + slot_index
    placement = jnp.arange(experts * capacity, dtype=jnp.int32)[:, None] == target[None, :]
    placed = placement.reshape(experts * capacity, token_count, TOP)
    dispatch_rows = jnp.any(placed, axis=2).astype(jnp.bfloat16)
    combine_rows = jnp.sum(jnp.where(placed, gate_values[None, :, :], 0.0), axis=2)
    outgoing = jnp.dot(dispatch_rows, normed, preferred_element_type=jnp.float32).astype(
        jnp.bfloat16
    )
    outgoing = outgoing.reshape(experts, capacity, D)
    doubled = jnp.broadcast_to(
        outgoing.reshape(experts, 1, capacity, D), (experts, 2, capacity, D)
    ).reshape(2 * experts, capacity, D)
    batch_in = lax.all_to_all(doubled, ("req", "wide"), split_axis=0, concat_axis=0, tiled=True)
    batch_shape = batch_in.shape
    flat_rows = batch_in.reshape(-1, D)
    gate_up = jnp.dot(flat_rows, expert_gate_up[0], preferred_element_type=jnp.float32)
    half_width = gate_up.shape[1] // 2
    activated = (jax.nn.silu(gate_up[:, :half_width]) * gate_up[:, half_width:]).astype(
        jnp.bfloat16
    )
    produced = jnp.dot(activated, expert_down[0], preferred_element_type=jnp.float32).astype(
        jnp.bfloat16
    )
    returned = lax.all_to_all(
        produced.reshape(batch_shape), ("req", "wide"), split_axis=0, concat_axis=0, tiled=True
    )
    halves = returned.reshape(experts, 2, capacity, D).astype(jnp.float32)
    summed_rows = (halves[:, 0] + halves[:, 1]).reshape(experts * capacity, D)
    mixture = lax.dot_general(
        combine_rows,
        summed_rows,
        (((0,), (0,)), ((), ())),
        precision=lax.Precision.HIGHEST,
        preferred_element_type=jnp.float32,
    )
    return (hidden_f32 + mixture).astype(jnp.bfloat16)


def solution(mesh):
    return jax.shard_map(
        body,
        mesh=mesh,
        in_specs=(
            P(("req", "wide"), None),
            P(("req", "wide"), None),
            P(None, ("req", "wide")),
            P(("req", "wide"), None),
            P("req", None, "wide", None),
            P("req", None, None, "wide"),
            P(("req", "wide"), None),
            P(("req", "wide"), None),
            P(),
            P(),
            P(),
            P(("req", "wide"), None),
            P(("req", "wide"), None),
            P(("req", "wide"), None, None),
            P(("req", "wide"), None, None),
        ),
        out_specs=P(("req", "wide"), None),
        check_vma=False,
    )
```

profile of v0, /device:TPU:0, one launch (start us, length us, event | category | flops | bytes accessed | tf_op | source)
XLA Modules:
  0.0 732.9 jit_solution(6475154528325271947)
XLA Ops:
  6.5 2.4 copy.133
  9.1 3.6 convolution_convert_fusion.2
  14.4 3.1 convolution_convert_fusion.3
  18.7 10.2 %all-gather = s32[8,1,128]{2,1,0:T(1,128)S(1)} all-gather(s32[1,1,128]{2,1,0:T(1,128)S(1)} %bitcast.195), channel_id=1, replica_groups=mesh['req'=4,'wide'=8] {'wide'}, dimensions={0}, use_global_device_ids=true | all-gather | bytes 4608 | tf_op jit(solution)/shard_map/all_gather | solution.py:92
  28.9 1.9 fusion.74
  30.9 27.8 %all-gather.3.cloned.1.call-done = bf16[1024,3072]{0,1:T(8,128)(2,1)} async-done(((bf16[128,3072]{0,1:T(8,128)(2,1)}), bf16[1024,3072]{0,1:T(8,128)(2,1)}) %all-gather.3.cloned.1.call-update) | async-done | bytes 6291472 | tf_op jit(solution)/shard_map/all_gather | solution.py:96
  58.6 4.7 slice.60
  63.3 3.1 slice.62
  66.4 80.4 %while.31 = (s32[]{:T(128)}, bf16[16,1024,128]{2,1,0:T(8,128)(2,1)}, bf16[16,1024]{1,0:T(8,128)(2,1)S(1)}, bf16[16,1024]{1,0:T(8,128)(2,1)S(1)}, bf16[16,1024,12...) while((s32[]{:T(128)}, ...), condition=%wide.region_10.11_spmd.clone, body=%wide.region_7.10_spmd.clone.sunk | while | flops 171310080 | bytes 6114949 | solution.py:65
  69.0 2.0 fusion.122
  74.0 2.0 fusion.122
  79.1 2.0 fusion.122
  84.1 2.0 fusion.122
  89.1 2.0 fusion.122
  94.1 2.0 fusion.122
  99.1 2.0 fusion.122
  104.2 2.0 fusion.122
  109.2 2.0 fusion.122
  114.2 2.0 fusion.122
  119.3 2.0 fusion.122
  124.3 2.0 fusion.122
  129.3 2.0 fusion.122
  134.3 2.0 fusion.122
  139.3 2.0 fusion.122
  144.4 2.0 fusion.122
  147.4 3.3 all-to-all-start
  151.4 4.2 all-to-all-done
  155.5 3.3 all-to-all-start.2
  158.9 2.3 fusion.75
  163.9 6.8 copy.147
  170.8 4.7 all-to-all-start.1
  175.5 116.7 %while.30 = (s32[]{:T(128)}, f32[16,128,128]{2,0,1:T(8,128)}, f32[16,128]{1,0:T(8,128)S(1)}, f32[16,128]{1,0:T(8,128)}, bf16[16,128,128]{1,2,0:T(8,128)(2,1)S(1)...) while((s32[]{:T(128)}, f32[16,128,128]{2,0,1:T(8,128)}, ...), condition=%wide.region_5.6_spmd.clone, body=%wide.region_2.5_spmd.clone.sunk | while | flops 10796802 | bytes 664193 | solution.py:124
  178.4 3.0 dynamic_update_slice.35
  185.8 3.0 dynamic_update_slice.35
  193.1 3.0 dynamic_update_slice.35
  200.5 3.0 dynamic_update_slice.35
  207.8 3.0 dynamic_update_slice.35
  215.2 3.0 dynamic_update_slice.35
  222.5 3.0 dynamic_update_slice.35
  229.8 3.0 dynamic_update_slice.35
  237.2 3.0 dynamic_update_slice.35
  244.4 3.0 dynamic_update_slice.35
  251.7 3.0 dynamic_update_slice.35
  258.9 3.0 dynamic_update_slice.35
  266.2 3.0 dynamic_update_slice.35
  273.4 3.0 dynamic_update_slice.35
  280.7 3.0 dynamic_update_slice.35
  287.9 3.0 dynamic_update_slice.35
  302.9 4.6 fusion.52
  308.2 4.8 multiply_reduce_fusion
  314.0 2.8 convolution_convert_fusion.4
  316.8 3.7 broadcast_in_dim.103
  320.5 3.2 broadcast_in_dim.104
  323.7 166.9 %all_to_all.33 = bf16[32,49,2048]{2,1,0:T(8,128)(2,1)} all-to-all(bf16[32,49,2048]{2,1,0:T(8,128)(2,1)S(1)} %bitcast.180), channel_id=1, replica_groups=mesh['req'=4,'wide'=8] {'req','wide'}, dimensions={0} | all-to-all | bytes 12845056 | tf_op jit(solution)/shard_map/all_to_all | solution.py:159
  490.6 7.0 reshape.162
  497.6 13.9 %fusion.54 = f32[1568,1408]{1,0:T(8,128)S(1)} fusion(bf16[1568,2048]{1,0:T(8,128)(2,1)} %reshape.162, bf16[1,2048,1408]{2,1,0:T(8,128)(2,1)} %param.32), kind=kOutput, calls=%fused_computation.60 | convolution fusion | flops 9042919424 | bytes 21020672 | tf_op jit(solution)/shard_map/dot_general | solution.py:162
  511.5 7.4 %convolution_convert_fusion.1 = bf16[1568,2048]{1,0:T(8,128)(2,1)} fusion(bf16[1,704,2048]{2,1,0:T(8,128)(2,1)S(1)} %copy-done, f32[1568,1408]{1,0:T(8,128)S(1)} %fusion.54), kind=kOutput, calls=%fused_computation.56 | convolution fusion | flops 4531294208 | bytes 18939904 | tf_op jit(solution)/shard_map/dot_general | solution.py:167
  518.9 7.0 reshape.163
  525.9 4.2 all-to-all-start.4
  530.4 162.7 %all-to-all-done.4 = bf16[32,49,2048]{2,1,0:T(8,128)(2,1)} async-done(((bf16[32,49,2048]{2,1,0:T(8,128)(2,1)}), bf16[32,49,2048]{2,1,0:T(8,128)(2,1)}, u32[]{:S(2)}, u32[]{:S(2)}) %all-to-all-start.4) | async-done | bytes 6422560 | tf_op jit(solution)/shard_map/all_to_all | solution.py:170
  693.1 10.1 %convert.4 = f32[16,2,49,2048]{3,2,1,0:T(8,128)} convert(bf16[16,2,49,2048]{3,2,1,0:T(8,128)(2,1)} %bitcast.27) | non-fusion elementwise | flops 3211264 | bytes 19267584 | tf_op jit(solution)/shard_map/convert_element_type | solution.py:173
  703.2 10.4 %fusion.53 = f32[16,1,49,2048]{3,2,0,1:T(8,128)} fusion(f32[16,2,49,2048]{3,2,1,0:T(8,128)} %convert.4), kind=kLoop, calls=%fused_computation.58 | loop fusion | flops 1605632 | bytes 19267584 | tf_op jit(solution)/shard_map/add | solution.py:174
  713.6 5.3 add.64
  718.8 7.2 fusion.62
  (296 shorter events, 135.7 us)
Async XLA Ops:
  6.5 505.0 %copy-start = (bf16[1,704,2048]{2,1,0:T(8,128)(2,1)S(1)}, bf16[1,704,2048]{2,1,0:T(8,128)(2,1)}, u32[]{:S(2)}) copy-start(bf16[1,704,2048]{2,1,0:T(8,128)(2,1)} %param.33) | copy-start | bytes 8650756
  6.5 52.1 %all-gather.3.cloned.1.call-start = ((), (), s32[]{:S(2)}) async-start(), calls=%async_computation.5 | async-start | bytes 7077888 | tf_op jit(solution)/shard_map/all_gather | solution.py:96
  9.0 5.2 copy-start.12
  9.0 5.3 copy-start.9
  12.6 6.0 copy-start.13
  12.6 16.3 %copy-start.10 = (bf16[1,2,64,128]{3,2,1,0:T(8,128)(2,1)S(1)}, bf16[1,2,64,128]{3,2,1,0:T(8,128)(2,1)}, u32[]{:S(2)}) copy-start(bf16[1,2,64,128]{3,2,1,0:T(8,128)(2,1)} %param.24) | copy-start | bytes 98308
  14.4 14.6 %copy-start.2 = (bf16[32,16,8,256]{3,2,0,1:T(8,128)(2,1)S(1)}, bf16[32,16,8,256]{3,2,0,1:T(8,128)(2,1)}, u32[]{:S(2)}) copy-start(bf16[32,16,8,256]{3,2,0,1:T(8,128)(2,1)} %copy.185) | copy-start | bytes 6291460
  147.4 8.1 %all-to-all-start = ((bf16[16,8,128]{2,0,1:T(8,128)(2,1)}), bf16[16,8,128]{2,0,1:T(8,128)(2,1)S(1)}, u32[]{:S(2)}, u32[]{:S(2)}) async-start(bf16[16,8,128]{2,0,1:T(8,128)(2,1)} %copy_bitcast_fusion.2), calls=%async_computation | async-start | bytes 65536 | tf_op jit(solution)/shard_map/all_to_all | solution.py:102
  155.5 15.2 %copy-start.5 = (bf16[16,8,128]{2,0,1:T(8,128)(2,1)}, bf16[16,8,128]{2,0,1:T(8,128)(2,1)S(1)}, u32[]{:S(2)}) copy-start(bf16[16,8,128]{2,0,1:T(8,128)(2,1)S(1)} %all-to-all-done) | copy-start | bytes 98308
  155.5 15.2 %all-to-all-start.2 = ((bf16[16,8,128]{2,0,1:T(8,128)(2,1)}), bf16[16,8,128]{2,0,1:T(8,128)(2,1)S(1)}, u32[]{:S(2)}, u32[]{:S(2)}) async-start(bf16[16,8,128]{2,0,1:T(8,128)(2,1)} %copy_bitcast_fusion.1), calls=%async_computation.2 | async-start | bytes 65536 | tf_op jit(solution)/shard_map/all_to_all | solution.py:103
  170.7 4.8 copy-start.8
  170.8 132.1 %all-to-all-start.1 = ((bf16[16,1024,128]{2,0,1:T(8,128)(2,1)}), bf16[16,1024,128]{2,0,1:T(8,128)(2,1)}, u32[]{:S(2)}, u32[]{:S(2)}) async-start(bf16[16,1024,128]{2,0,1:T(8,128)(2,1)} %copy.147), calls=%async_computation.1 | async-start | bytes 8388608 | tf_op jit(solution)/shard_map/all_to_all | solution.py:101
  302.8 4.6 copy-start.3
  302.8 4.6 copy-start.6
  302.8 4.6 copy-start.7
  302.9 5.4 copy-start.4
  313.0 1.0 copy-start.1
  525.9 4.2 copy-start.11
  525.9 167.2 %all-to-all-start.4 = ((bf16[32,49,2048]{2,1,0:T(8,128)(2,1)}), bf16[32,49,2048]{2,1,0:T(8,128)(2,1)}, u32[]{:S(2)}, u32[]{:S(2)}) async-start(bf16[32,49,2048]{2,1,0:T(8,128)(2,1)} %reshape.163), calls=%async_computation.4 | async-start | bytes 14680064 | tf_op jit(solution)/shard_map/all_to_all | solution.py:170
Sparse Core Ops, SparseCore 0:
  9.2 49.3 all-gather.2
where the time goes:
time: 739 us; the launch traced here: 733 us
  waiting for transfers between devices  195 us (26%)
  blocking collectives  177 us (24%)
  matrix products  162 us (22%)
  local copies, waits for them, and re-layouts  130 us (18%)
  other arithmetic  38.6 us (5%)
  starting transfers between devices  15.6 us (2%)
  between operations  13.7 us (2%)
    all_to_all x1, blocking collectives, body(): lax.all_to_all(doubled, ('req', 'wide'), split_axis=0, concat_axis=0, til...  167 us
    all_to_all x1, waiting for transfers between devices, body(): lax.all_to_all(produced.reshape(batch_shape), ('req', 'wide'), split_axis...  163 us
    dynamic_update_slice x48, local copies, waits for them, and re-layouts, body(): lax.map(local_head, (query_nope, query_rope, suffix_keys, suffix_values))  68.7 us
    dot_general x32, matrix products, head_scores(): rotary = jnp.dot(head_rope, rope_keys, preferred_element_type=jnp.float32)  35.9 us
    dot_general x32, matrix products, head_scores(): lax.dot_general(head_nope, head_keys, (((1,), (1,)), ((), ())), preferred...  35.3 us
    dot_general x16, matrix products, one_head(): jnp.dot(weights.astype(jnp.bfloat16), head_values, preferred_element_type...  32 us
    all_gather x1, waiting for transfers between devices, body(): lax.all_gather(queries, 'wide', axis=0, tiled=True)  27.8 us
    dot_general x16, matrix products, local_head(): jnp.dot(weights.astype(jnp.bfloat16), head_values, preferred_element_type...  16.3 us
  transfers between devices with their start and end apart: 5, of which 3 were waited for; matrix products, arithmetic and copies ran while one was open for 21% of the time, Pallas kernels for 0%

commit v1 on v0

v1 whole, which is shorter than its diff:
```python
import functools

import jax
import jax.numpy as jnp
from jax import lax
from jax.experimental import pallas as pl
from jax.experimental.pallas import tpu as pltpu
from jax.sharding import PartitionSpec as P

D = 2048
HEADS = 16
NOPE = 128
ROPE = 64
LAT = 512
TOP = 6
PREF = 2
KEY = 640
STACK = 4


epsilon = 1e-06


def request_tables(lengths, request_ids, token_count):
    request_end = jnp.cumsum(lengths)
    positions = jnp.arange(token_count, dtype=jnp.int32)
    segment = jnp.sum((positions[:, None] >= request_end[None, :]).astype(jnp.int32), axis=1)
    matches = segment[:, None] == jnp.arange(request_ids.shape[0], dtype=jnp.int32)[None, :]
    prefix = jnp.sum(jnp.where(matches, request_ids[None, :], 0), axis=1)
    return (segment, prefix)


def joined_keys(latent, rope_columns):
    rope_rows = rope_columns.T
    padding = jnp.zeros((latent.shape[0], KEY - LAT - ROPE), latent.dtype)
    return jnp.concatenate([latent, rope_rows, padding], axis=1)


def contract_last(left, right):
    return lax.dot_general(
        left, right, (((1,), (1,)), ((), ())), preferred_element_type=jnp.float32
    )


def attention_kernel(
    wide_count,
    query_ref,
    rope_ref,
    own_ref,
    local_ref,
    bias_ref,
    w_ref,
    out_ref,
    keys,
    absorbed,
    send_sem,
    recv_sem,
    pass_sem,
    land_sem,
):
    me = lax.axis_index("wide")
    rows = own_ref.shape[0]
    tokens = query_ref.shape[0]
    far_rows = keys.shape[0]
    scaling = 1.0 / (NOPE + ROPE) ** 0.5
    half = wide_count // 2
    sibling = me + 1 - 2 * lax.rem(me, 2)
    slot = lambda owner: pl.ds(pl.multiple_of(owner * rows, rows), rows)

    barrier = pltpu.get_barrier_semaphore()
    peers = [sibling] + [lax.rem(me + 2 * k, wide_count) for k in range(1, half)]
    for peer in peers:
        pl.semaphore_signal(
            barrier, inc=1, device_id={"wide": peer}, device_id_type=pl.DeviceIdType.MESH
        )
    pl.semaphore_wait(barrier, half)

    first = []
    for k, peer in enumerate(peers):
        copy = pltpu.make_async_remote_copy(
            src_ref=own_ref,
            dst_ref=keys.at[slot(me)],
            send_sem=send_sem.at[k],
            recv_sem=recv_sem.at[k],
            device_id={"wide": peer},
            device_id_type=pl.DeviceIdType.MESH,
        )
        copy.start()
        first.append(copy)
    keys[slot(me), :] = own_ref[...]

    def absorb(group, carry):
        start = pl.multiple_of(group * STACK * NOPE, STACK * NOPE)
        query = query_ref[:, pl.ds(start, STACK * NOPE)]
        rope = rope_ref[:, pl.ds(start, STACK * NOPE)]
        weights = w_ref[:, pl.ds(pl.multiple_of(2 * start, 2 * STACK * NOPE), 2 * STACK * NOPE)]
        base = pl.multiple_of(group * STACK * tokens, STACK * tokens)
        for j in range(STACK):
            product = contract_last(
                query[:, j * NOPE : (j + 1) * NOPE],
                weights[:, 2 * j * NOPE : (2 * j + 1) * NOPE],
            ).astype(jnp.bfloat16)
            absorbed[pl.ds(base + j * tokens, tokens), 0:LAT] = product
            absorbed[pl.ds(base + j * tokens, tokens), LAT:KEY] = rope[
                :, j * NOPE : (j + 1) * NOPE
            ]
        return carry

    lax.fori_loop(0, HEADS // STACK, absorb, 0)

    second = []
    for k in range(1, half):
        first[k].wait_recv()
        source = lax.rem(me + wide_count - 2 * k, wide_count)
        copy = pltpu.make_async_remote_copy(
            src_ref=keys.at[slot(source)],
            dst_ref=keys.at[slot(source)],
            send_sem=pass_sem.at[k - 1],
            recv_sem=land_sem.at[k - 1],
            device_id={"wide": sibling},
            device_id_type=pl.DeviceIdType.MESH,
        )
        copy.start()
        second.append(copy)
    first[0].wait_recv()
    for copy in second:
        copy.wait_recv()

    def attend(group, carry):
        base = pl.multiple_of(group * STACK * tokens, STACK * tokens)
        query = absorbed[pl.ds(base, STACK * tokens), :]
        far = contract_last(query, keys[...]).reshape(STACK, tokens, far_rows)
        near = contract_last(query, local_ref[...]).reshape(STACK, tokens, tokens)
        far = far + bias_ref[:, 0:far_rows][None]
        near = near + bias_ref[:, far_rows:][None]
        largest = jnp.maximum(
            jnp.max(far, axis=2, keepdims=True), jnp.max(near, axis=2, keepdims=True)
        )
        far = jnp.exp((far - largest) * scaling)
        near = jnp.exp((near - largest) * scaling)
        total = jnp.sum(far, axis=2, keepdims=True) + jnp.sum(near, axis=2, keepdims=True)
        far16 = far.astype(jnp.bfloat16).reshape(STACK * tokens, far_rows)
        near16 = near.astype(jnp.bfloat16).reshape(STACK * tokens, tokens)
        mixed = jnp.dot(far16, keys[:, 0:LAT], preferred_element_type=jnp.float32)
        mixed = mixed + jnp.dot(near16, local_ref[:, 0:LAT], preferred_element_type=jnp.float32)
        mixed = (mixed / total.reshape(STACK * tokens, 1)).astype(jnp.bfloat16)
        start = pl.multiple_of(group * STACK * NOPE, STACK * NOPE)
        weights = w_ref[:, pl.ds(pl.multiple_of(2 * start, 2 * STACK * NOPE), 2 * STACK * NOPE)]
        parts = []
        for j in range(STACK):
            parts.append(
                jnp.dot(
                    mixed[j * tokens : (j + 1) * tokens],
                    weights[:, (2 * j + 1) * NOPE : (2 * j + 2) * NOPE],
                    preferred_element_type=jnp.float32,
                ).astype(jnp.bfloat16)
            )
        out_ref[:, pl.ds(start, STACK * NOPE)] = jnp.concatenate(parts, axis=1)
        return carry

    lax.fori_loop(0, HEADS // STACK, attend, 0)
    for copy in first + second:
        copy.wait_send()


def attention(queries, suffix_latent, suffix_rope, prefix_latent, prefix_rope, segment, prefix, w_ukv):
    token_count = queries.shape[0]
    wide_count = lax.axis_size("wide")
    half = wide_count // 2
    block_rows = prefix_latent.shape[2]
    rows = PREF * block_rows
    own = joined_keys(
        prefix_latent[0].reshape(rows, LAT),
        prefix_rope[0].transpose(1, 0, 2).reshape(ROPE, rows),
    )
    local = joined_keys(suffix_latent, suffix_rope)
    query_rope = queries[:, HEADS * NOPE :].reshape(token_count, HEADS, ROPE)
    query_rope = jnp.pad(query_rope, ((0, 0), (0, 0), (0, NOPE - ROPE)))
    query_rope = query_rope.reshape(token_count, HEADS * NOPE)
    positions = jnp.arange(token_count, dtype=jnp.int32)
    causal = (segment[:, None] == segment[None, :]) & (positions[None, :] <= positions[:, None])
    key_owner = jnp.tile(jnp.repeat(jnp.arange(PREF, dtype=jnp.int32), block_rows), wide_count)
    allowed = jnp.concatenate([prefix[:, None] == key_owner[None, :], causal], axis=1)
    bias = jnp.where(allowed, 0.0, -jnp.inf).astype(jnp.float32)
    vmem = pl.BlockSpec(memory_space=pltpu.VMEM)
    return pl.pallas_call(
        functools.partial(attention_kernel, wide_count),
        out_shape=jax.ShapeDtypeStruct((token_count, HEADS * NOPE), jnp.bfloat16),
        in_specs=[vmem] * 6,
        out_specs=vmem,
        scratch_shapes=[
            pltpu.VMEM((wide_count * rows, KEY), jnp.bfloat16),
            pltpu.VMEM((HEADS * token_count, KEY), jnp.bfloat16),
            pltpu.SemaphoreType.DMA((half,)),
            pltpu.SemaphoreType.DMA((half,)),
            pltpu.SemaphoreType.DMA((half - 1,)),
            pltpu.SemaphoreType.DMA((half - 1,)),
        ],
        compiler_params=pltpu.CompilerParams(
            collective_id=0, has_side_effects=True, vmem_limit_bytes=52 * 2**20
        ),
    )(queries[:, : HEADS * NOPE], query_rope, own, local, bias, w_ukv)


def expert_half(rows, gate_up_weights, down_weights):
    gate_up = jnp.dot(rows, gate_up_weights, preferred_element_type=jnp.float32)
    half_width = gate_up.shape[1] // 2
    activated = (jax.nn.silu(gate_up[:, :half_width]) * gate_up[:, half_width:]).astype(
        jnp.bfloat16
    )
    return jnp.dot(activated, down_weights, preferred_element_type=jnp.float32).astype(
        jnp.bfloat16
    )


def body(
    queries,
    suffix_latent,
    suffix_rope,
    residual,
    prefix_latent,
    prefix_rope,
    suffix_lengths,
    prefix_ids,
    w_ukv,
    w_out,
    norm_gain,
    expert_ids,
    gate_values,
    expert_gate_up,
    expert_down,
):
    token_count = queries.shape[0]
    req_count = lax.axis_size("req")
    wide_count = lax.axis_size("wide")
    devices = req_count * wide_count
    segment, prefix = request_tables(suffix_lengths[0], prefix_ids[0], token_count)
    head_out = attention(
        queries, suffix_latent, suffix_rope, prefix_latent, prefix_rope, segment, prefix, w_ukv
    )
    projected = jnp.dot(head_out, w_out, preferred_element_type=jnp.float32)
    hidden = (residual.astype(jnp.float32) + projected).astype(jnp.bfloat16)
    hidden_f32 = hidden.astype(jnp.float32)
    inverse = lax.rsqrt(jnp.mean(hidden_f32 * hidden_f32, axis=1, keepdims=True) + epsilon)
    normed = (hidden_f32 * inverse * norm_gain.astype(jnp.float32)[None, :]).astype(jnp.bfloat16)

    experts = devices // 2
    share = (token_count * TOP // experts + 2) // 2
    capacity = 2 * share
    flat_ids = expert_ids.reshape(-1)
    one_hot = (flat_ids[:, None] == jnp.arange(experts, dtype=jnp.int32)[None, :]).astype(jnp.int32)
    slot_index = jnp.sum((jnp.cumsum(one_hot, axis=0) - 1) * one_hot, axis=1)
    target = (flat_ids * capacity + slot_index).reshape(token_count, TOP)
    slots = jnp.arange(experts * capacity, dtype=jnp.int32)
    placed = [slots[:, None] == target[None, :, k] for k in range(TOP)]
    dispatch_rows = functools.reduce(jnp.logical_or, placed).astype(jnp.bfloat16)
    combine_rows = sum(
        jnp.where(placed[k], gate_values[None, :, k], 0.0) for k in range(TOP)
    )
    combine_high = combine_rows.astype(jnp.bfloat16)
    combine_low = (combine_rows - combine_high.astype(jnp.float32)).astype(jnp.bfloat16)
    outgoing = jnp.dot(dispatch_rows, normed, preferred_element_type=jnp.float32).astype(
        jnp.bfloat16
    )
    lanes = D // 128
    swap = [(i, i ^ 1) for i in range(wide_count)]

    def exchange(rows):
        moved = lax.all_to_all(
            rows.reshape(devices, share, lanes, 128),
            ("req", "wide"),
            split_axis=0,
            concat_axis=0,
            tiled=True,
        )
        return moved.reshape(devices * share, D)

    own_rows = exchange(outgoing)
    other_rows = lax.ppermute(own_rows, "wide", swap)
    own_half = expert_half(own_rows, expert_gate_up[0], expert_down[0])
    other_half = expert_half(other_rows, expert_gate_up[0], expert_down[0])
    arrived = lax.ppermute(other_half, "wide", swap)
    summed = (own_half.astype(jnp.float32) + arrived.astype(jnp.float32)).astype(jnp.bfloat16)
    returned = exchange(summed)
    both = jnp.concatenate([combine_high, combine_low], axis=1)
    mixture = lax.dot_general(
        both, returned, (((0,), (0,)), ((), ())), preferred_element_type=jnp.float32
    )
    mixture = mixture[:token_count] + mixture[token_count:]
    return (hidden_f32 + mixture).astype(jnp.bfloat16)


def solution(mesh):
    return jax.shard_map(
        body,
        mesh=mesh,
        in_specs=(
            P(("req", "wide"), None),
            P(("req", "wide"), None),
            P(None, ("req", "wide")),
            P(("req", "wide"), None),
            P("req", None, "wide", None),
            P("req", None, None, "wide"),
            P(("req", "wide"), None),
            P(("req", "wide"), None),
            P(),
            P(),
            P(),
            P(("req", "wide"), None),
            P(("req", "wide"), None),
            P(("req", "wide"), None, None),
            P(("req", "wide"), None, None),
        ),
        out_specs=P(("req", "wide"), None),
        check_vma=False,
    )
```

time: 739 us -> 270 us (0.37)
  matrix products: 162 us -> 26 us
  waiting for transfers between devices: 195 us -> 80.3 us
  local copies, waits for them, and re-layouts: 130 us -> 18.2 us
  blocking collectives: 177 us -> 81.2 us
  Pallas kernels: 0 us -> 49.4 us
  other arithmetic: 38.6 us -> 10.1 us
  between operations: 13.7 us -> 0.27 us
  starting transfers between devices: 15.6 us -> 3.94 us
    dot_general x102 -> x6, matrix products: 159 us -> 24.8 us  [the longest x2 10.5 us: expert_half(): gate_up = jnp.dot(rows, gate_up_weights, preferred_element_type=jnp.float32)]
    all_to_all x4 -> x1, waiting for transfers between devices: 167 us -> 74 us  [exchange(): lax.all_to_all(rows.reshape(devices, share, lanes, 128), ('req', 'wide'),...]
    all_to_all x1, blocking collectives: 167 us -> 81.2 us  [exchange(): lax.all_to_all(rows.reshape(devices, share, lanes, 128), ('req', 'wide'),...]
    dynamic_update_slice x80 -> x0, local copies, waits for them, and re-layouts: 70.9 us -> none  [the longest x48 68.7 us: body(): lax.map(local_head, (query_nope, query_rope, suffix_keys, suffix_values))]
    pallas_call x0 -> x1, Pallas kernels: none -> 49.4 us  [attention(): pl.pallas_call(functools.partial(attention_kernel, wide_count), out_shape...]
    all_gather x1 -> x0, waiting for transfers between devices: 27.8 us -> none  [body(): lax.all_gather(queries, 'wide', axis=0, tiled=True)]
    reshape x5 -> x1, local copies, waits for them, and re-layouts: 16.6 us -> 2.06 us  [attention(): query_rope = query_rope.reshape(token_count, HEADS * NOPE)]
    slice x7 -> x3, local copies, waits for them, and re-layouts: 15 us -> 3 us  [the longest x1 1.67 us: attention(): query_rope = queries[:, HEADS * NOPE:].reshape(token_count, HEADS, ROPE)]
  transfers between devices with their start and end apart: 5 -> 3, of which waited for: 3 -> 3; matrix products, arithmetic and copies ran while one was open for 21% -> 2% of each run, Pallas kernels for 0% -> 0%
where the time goes in v1:
time: 270 us; the launch traced here: 269 us
  blocking collectives  81.2 us (30%)
  waiting for transfers between devices  80.3 us (30%)
  Pallas kernels  49.4 us (18%)
  matrix products  26 us (10%)
  local copies, waits for them, and re-layouts  18.2 us (7%)
  other arithmetic  10.1 us (4%)
  starting transfers between devices  3.94 us (1%)
    all_to_all x1, blocking collectives, exchange(): lax.all_to_all(rows.reshape(devices, share, lanes, 128), ('req', 'wide'),...  81.2 us
    all_to_all x1, waiting for transfers between devices, exchange(): lax.all_to_all(rows.reshape(devices, share, lanes, 128), ('req', 'wide'),...  74 us
    pallas_call x1, Pallas kernels, attention(): pl.pallas_call(functools.partial(attention_kernel, wide_count), out_shape...  49.4 us
    dot_general x2, matrix products, expert_half(): gate_up = jnp.dot(rows, gate_up_weights, preferred_element_type=jnp.float32)  10.5 us
    unnamed x24, local copies, waits for them, and re-layouts  9.94 us
    dot_general x2, matrix products, expert_half(): jnp.dot(activated, down_weights, preferred_element_type=jnp.float32)  6.27 us
    ppermute x1, waiting for transfers between devices, body(): other_rows = lax.ppermute(own_rows, 'wide', swap)  5.83 us
  transfers between devices with their start and end apart: 3, of which 3 were waited for; matrix products, arithmetic and copies ran while one was open for 2% of the time, Pallas kernels for 0%

profile of v1, /device:TPU:0, one launch (start us, length us, event | category | flops | bytes accessed | tf_op | source)
XLA Modules:
  0.0 269.4 jit_solution(2743357068623347478)
XLA Ops:
  0.0 0.0 copy-start
  0.0 0.9 copy.49
  0.9 0.1 eq.171
  1.1 0.1 eq.167
  1.2 1.7 slice.67
  2.9 1.1 slice.66.query_ref
  4.0 1.7 reduce-window.19
  5.7 0.3 slice_reduce_fusion
  6.0 0.1 fusion.43
  6.1 0.1 reduce_sum.41
  6.2 0.1 copy.52
  6.3 0.7 multiply_add_fusion
  7.0 0.8 reduce-window.18
  7.8 0.1 convert_reduce_fusion
  7.9 0.1 fusion.41
  8.0 1.3 select_reduce_fusion
  9.3 0.9 copy.47
  10.2 0.8 copy.48
  11.1 1.8 copy.54
  12.8 1.8 pad.4
  14.7 2.1 copy.53.rope_ref
  16.7 0.9 broadcast_compare_fusion
  17.6 1.1 add_select_fusion.bias_ref
  18.7 0.1 pad.14.clone
  18.8 1.0 maximum_maximum_fusion.own_ref
  19.8 0.9 maximum_maximum_fusion.1.local_ref
  20.7 0.0 copy-start.3
  20.8 49.4 %shard_map.145 = bf16[128,2048]{1,0:T(8,128)(2,1)S(1)} custom-call(bf16[128,2048]{1,0:T(8,128)(2,1)S(1)} %slice.66.query_ref, bf16[128,2048]{1,0:T(8,128)(2,1)} %copy.53.rope_ref, bf16[256,640]{1,0:T(8,128)(2,1)S(1)} %maximum_maximum_fusion.own_ref, bf16[128,640]{1,0:T(8,128)(2,1)S(1)} %maximum_maximum_fusion.1.local_ref, ...), custom_call_target="tpu_custom_call" | custom-call | tf_op jit(solution)/shard_map/pallas_call | solution.py:186
  70.2 0.0 copy-done.3
  70.2 0.0 copy-start.4
  70.2 4.8 %multiply_reduce_fusion = (f32[128]{0:T(128)S(1)}, f32[128,2048]{1,0:T(8,128)S(1)}) fusion(bf16[128,2048]{1,0:T(8,128)(2,1)S(1)} %shard_map.145, bf16[2048,2048]{1,0:T(8,128)(2,1)} %param.24, bf16[128,2048]{1,0:T(8,128)(2,1)S(1)} %copy-done.3), kind=kOutput, calls=%fused_computation.30 | convolution fusion | flops 1075314560 | bytes 10486272 | tf_op jit(solution)/shard_map/dot_general | solution.py:241
  75.0 0.0 copy-start.1
  75.0 0.0 copy-done.4
  75.0 1.0 copy-done.1
  76.0 1.1 fusion.14
  77.2 0.0 slice-start
  77.2 1.0 copy.57
  78.2 0.0 slice-start.1
  78.2 81.2 %all_to_all.10 = bf16[32,25,16,128]{3,2,1,0:T(8,128)(2,1)S(1)} all-to-all(bf16[32,25,16,128]{3,2,1,0:T(8,128)(2,1)S(1)} %bitcast.95), channel_id=1, replica_groups=mesh['req'=4,'wide'=8] {'req','wide'}, dimensions={0} | all-to-all | bytes 6553600 | tf_op jit(solution)/shard_map/all_to_all | solution.py:269
  159.4 1.5 copy.68
  161.0 0.1 collective-permute-start
  161.1 5.8 %collective-permute-done = bf16[800,2048]{1,0:T(8,128)(2,1)S(1)} collective-permute-done((bf16[800,2048]{1,0:T(8,128)(2,1)S(1)}, bf16[800,2048]{1,0:T(8,128)(2,1)S(1)}, u32[]{:S(2)}, u32[]{:S(2)}) %collective-permute-start) | collective-permute-done | bytes 3276832 | tf_op jit(solution)/shard_map/ppermute | solution.py:279
  166.9 0.0 slice-done
  166.9 0.0 slice-done.1
  166.9 5.2 %fusion = f32[800,1408]{1,0:T(8,128)S(1)} fusion(bf16[800,2048]{1,0:T(8,128)(2,1)S(1)} %collective-permute-done, bf16[1,2048,1408]{2,1,0:T(8,128)(2,1)S(1)} %bitcast.106), kind=kOutput, calls=%fused_computation.1 | convolution fusion | flops 4613734400 | bytes 13549568 | tf_op jit(solution)/shard_map/dot_general | solution.py:206
  172.1 0.0 copy-done
  172.2 3.1 %convolution_convert_fusion.1 = bf16[800,2048]{1,0:T(8,128)(2,1)S(1)} fusion(bf16[1,704,2048]{2,1,0:T(8,128)(2,1)S(1)} %copy-done, f32[800,1408]{1,0:T(8,128)S(1)} %fusion), kind=kOutput, calls=%fused_computation.6 | convolution fusion | flops 2311884800 | bytes 11075584 | tf_op jit(solution)/shard_map/dot_general | solution.py:211
  175.3 0.2 collective-permute-start.1
  175.5 5.2 %fusion.2 = f32[800,1408]{1,0:T(8,128)S(1)} fusion(bf16[1,2048,1408]{2,1,0:T(8,128)(2,1)S(1)} %bitcast.106, bf16[100,8,16,128]{3,2,1,0:T(8,128)(2,1)S(1)} %bitcast.94), kind=kOutput, calls=%fused_computation.3 | convolution fusion | flops 4613734400 | bytes 13549568 | tf_op jit(solution)/shard_map/dot_general | solution.py:206
  180.7 0.5 collective-permute-done.1
  181.2 3.2 %fusion.4 = bf16[100,8,16,128]{3,1,2,0:T(8,128)(2,1)S(1)} fusion(bf16[800,2048]{1,0:T(8,128)(2,1)S(1)} %collective-permute-done.1, bf16[1,704,2048]{2,1,0:T(8,128)(2,1)S(1)} %copy-done, f32[800,1408]{1,0:T(8,128)S(1)} %fusion.2), kind=kOutput, calls=%fused_computation.8 | convolution fusion | flops 2318438400 | bytes 14352384 | tf_op jit(solution)/shard_map/dot_general | solution.py:211
  184.4 2.8 %copy.59 = bf16[100,8,16,128]{3,2,1,0:T(8,128)(2,1)} copy(bf16[100,8,16,128]{3,1,2,0:T(8,128)(2,1)S(1)} %fusion.4) | data formatting | bytes 6553600
  187.1 0.0 copy-start.5
  187.1 3.7 %all-to-all-start.1 = ((bf16[32,25,16,128]{3,2,1,0:T(8,128)(2,1)}), bf16[32,25,16,128]{3,2,1,0:T(8,128)(2,1)}, u32[]{:S(2)}, u32[]{:S(2)}) async-start(bf16[32,25,16,128]{3,2,1,0:T(8,128)(2,1)} %bitcast.92), calls=%async_computation.1 | async-start | bytes 6553600 | tf_op jit(solution)/shard_map/all_to_all | solution.py:269
  190.8 0.0 copy-done.5
  190.8 0.3 subtract_convert_fusion
  191.1 74.0 %all-to-all-done.1 = bf16[32,25,16,128]{3,2,1,0:T(8,128)(2,1)} async-done(((bf16[32,25,16,128]{3,2,1,0:T(8,128)(2,1)}), bf16[32,25,16,128]{3,2,1,0:T(8,128)(2,1)}, u32[]{:S(2)}, u32[]{:S(2)}) %all-to-all-start.1) | async-done | bytes 3276832 | tf_op jit(solution)/shard_map/all_to_all | solution.py:269
  265.1 0.0 copy-start.2
  265.1 3.3 %fusion.5 = f32[256,2048]{1,0:T(8,128)S(1)} fusion(bf16[100,8,16,128]{3,2,1,0:T(8,128)(2,1)} %bitcast.43, bf16[800,128]{1,0:T(8,128)(2,1)S(1)} %get-tuple-element.5, bf16[800,128]{1,0:T(8,128)(2,1)S(1)} %get-tuple-element.6), kind=kOutput, calls=%fused_computation.9 | convolution fusion | flops 839680000 | bytes 5783552 | tf_op jit(solution)/shard_map/dot_general | solution.py:286
  268.4 0.0 copy-done.2
  268.4 1.0 fusion.22
  (11 shorter events, 0.1 us)
Async XLA Ops:
  0.0 172.1 %copy-start = (bf16[1,704,2048]{2,1,0:T(8,128)(2,1)S(1)}, bf16[1,704,2048]{2,1,0:T(8,128)(2,1)}, u32[]{:S(2)}) copy-start(bf16[1,704,2048]{2,1,0:T(8,128)(2,1)} %param.29) | copy-start | bytes 8650756
  20.7 49.4 %copy-start.3 = (bf16[128,2048]{1,0:T(8,128)(2,1)S(1)}, bf16[128,2048]{1,0:T(8,128)(2,1)}, u32[]{:S(2)}) copy-start(bf16[128,2048]{1,0:T(8,128)(2,1)} %param.18) | copy-start | bytes 1572868
  70.2 4.8 %copy-start.4 = (bf16[2048]{0:T(1024)(128)(2,1)S(1)}, bf16[2048]{0:T(1024)(128)(2,1)}, u32[]{:S(2)}) copy-start(bf16[2048]{0:T(1024)(128)(2,1)} %param.25) | copy-start | bytes 12292
  75.0 1.0 copy-start.1
  77.2 89.7 %slice-start = ((s8[5767168]{0:T(1024)(128)(4,1)}), s8[4194304]{0:T(1024)(128)(4,1)S(1)}, s32[]{:S(2)}) async-start(s8[5767168]{0:T(1024)(128)(4,1)} %bitcast.105), calls=%async_computation.2 | async-start | bytes 8388608
  78.2 88.7 %slice-start.1 = ((s8[5767168]{0:T(1024)(128)(4,1)}), s8[1572864]{0:T(1024)(128)(4,1)S(1)}, s32[]{:S(2)}) async-start(s8[5767168]{0:T(1024)(128)(4,1)} %bitcast.105), calls=%async_computation.3 | async-start | bytes 3145728
  161.0 5.9 %collective-permute-start = (bf16[800,2048]{1,0:T(8,128)(2,1)S(1)}, bf16[800,2048]{1,0:T(8,128)(2,1)S(1)}, u32[]{:S(2)}, u32[]{:S(2)}) collective-permute-start(bf16[800,2048]{1,0:T(8,128)(2,1)S(1)} %bitcast.96), channel_id=1, source_target_pairs={{0,1},{1,0},{2,3},{3,2},{4,5},{5,4},{6,7},{7,6},{8,9},{9,8},{10,11... | collective-permute-start | bytes 9830408 | tf_op jit(solution)/shard_map/ppermute | solution.py:279
  175.3 5.9 %collective-permute-start.1 = (bf16[800,2048]{1,0:T(8,128)(2,1)S(1)}, bf16[800,2048]{1,0:T(8,128)(2,1)S(1)}, u32[]{:S(2)}, u32[]{:S(2)}) collective-permute-start(bf16[800,2048]{1,0:T(8,128)(2,1)S(1)} %convolution_convert_fusion.1), channel_id=1, source_target_pairs={{0,1},{1,0},{2,3},{3,2},{4,5},{5,4},{6,7},{7,6},{8,9},{9,8},{10,11... | collective-permute-start | bytes 9830408 | tf_op jit(solution)/shard_map/ppermute | solution.py:282
  187.1 3.7 %copy-start.5 = (f32[128,6]{0,1:T(8,128)S(1)}, f32[128,6]{0,1:T(8,128)}, u32[]{:S(2)}) copy-start(f32[128,6]{0,1:T(8,128)} %param.27) | copy-start | bytes 9220
  187.1 78.0 %all-to-all-start.1 = ((bf16[32,25,16,128]{3,2,1,0:T(8,128)(2,1)}), bf16[32,25,16,128]{3,2,1,0:T(8,128)(2,1)}, u32[]{:S(2)}, u32[]{:S(2)}) async-start(bf16[32,25,16,128]{3,2,1,0:T(8,128)(2,1)} %bitcast.92), calls=%async_computation.1 | async-start | bytes 6553600 | tf_op jit(solution)/shard_map/all_to_all | solution.py:269
  265.1 3.3 %copy-start.2 = (f32[128,2048]{1,0:T(8,128)S(1)}, f32[128,2048]{1,0:T(8,128)}, u32[]{:S(2)}) copy-start(f32[128,2048]{1,0:T(8,128)} %copy-done.1) | copy-start | bytes 3145732

commit v2 on v1

--- a/solution.py
+++ b/solution.py
@@ -1,4 +1,5 @@
 import functools
+import math
 
 import jax
 import jax.numpy as jnp
@@ -32,8 +33,7 @@
 
 def joined_keys(latent, rope_columns):
     rope_rows = rope_columns.T
-    padding = jnp.zeros((latent.shape[0], KEY - LAT - ROPE), latent.dtype)
-    return jnp.concatenate([latent, rope_rows, padding], axis=1)
+    return jnp.concatenate([latent, rope_rows, rope_rows], axis=1)
 
 
 def contract_last(left, right):
@@ -45,7 +45,6 @@
 def attention_kernel(
     wide_count,
     query_ref,
-    rope_ref,
     own_ref,
     local_ref,
     bias_ref,
@@ -53,6 +52,9 @@
     out_ref,
     keys,
     absorbed,
+    total_out,
+    total_max,
+    total_sum,
     send_sem,
     recv_sem,
     pass_sem,
@@ -61,11 +63,10 @@
     me = lax.axis_index("wide")
     rows = own_ref.shape[0]
     tokens = query_ref.shape[0]
-    far_rows = keys.shape[0]
-    scaling = 1.0 / (NOPE + ROPE) ** 0.5
+    scaling = math.log2(math.e) / (NOPE + ROPE) ** 0.5
     half = wide_count // 2
     sibling = me + 1 - 2 * lax.rem(me, 2)
-    slot = lambda owner: pl.ds(pl.multiple_of(owner * rows, rows), rows)
+    slot = lambda place: pl.ds(place * rows, rows)
 
     barrier = pltpu.get_barrier_semaphore()
     peers = [sibling] + [lax.rem(me + 2 * k, wide_count) for k in range(1, half)]
@@ -79,7 +80,7 @@
     for k, peer in enumerate(peers):
         copy = pltpu.make_async_remote_copy(
             src_ref=own_ref,
-            dst_ref=keys.at[slot(me)],
+            dst_ref=keys.at[slot(2 * k if k else 1)],
             send_sem=send_sem.at[k],
             recv_sem=recv_sem.at[k],
             device_id={"wide": peer},
@@ -87,34 +88,78 @@
         )
         copy.start()
         first.append(copy)
-    keys[slot(me), :] = own_ref[...]
+    keys[slot(0), :] = own_ref[...]
+    low = lax.broadcasted_iota(jnp.int32, (tokens, NOPE), 1) < ROPE
+
+    def group_weights(group):
+        width = 2 * STACK * NOPE
+        return w_ref[:, pl.ds(pl.multiple_of(group * width, width), width)]
 
     def absorb(group, carry):
-        start = pl.multiple_of(group * STACK * NOPE, STACK * NOPE)
-        query = query_ref[:, pl.ds(start, STACK * NOPE)]
-        rope = rope_ref[:, pl.ds(start, STACK * NOPE)]
-        weights = w_ref[:, pl.ds(pl.multiple_of(2 * start, 2 * STACK * NOPE), 2 * STACK * NOPE)]
+        query = query_ref[:, pl.ds(pl.multiple_of(group * STACK * NOPE, NOPE), STACK * NOPE)]
+        rope_start = pl.multiple_of(HEADS * NOPE + group * STACK * ROPE, NOPE)
+        rope = query_ref[:, pl.ds(rope_start, STACK * ROPE)].astype(jnp.float32) * scaling
+        weights = group_weights(group)
         base = pl.multiple_of(group * STACK * tokens, STACK * tokens)
         for j in range(STACK):
             product = contract_last(
                 query[:, j * NOPE : (j + 1) * NOPE],
                 weights[:, 2 * j * NOPE : (2 * j + 1) * NOPE],
-            ).astype(jnp.bfloat16)
-            absorbed[pl.ds(base + j * tokens, tokens), 0:LAT] = product
-            absorbed[pl.ds(base + j * tokens, tokens), LAT:KEY] = rope[
-                :, j * NOPE : (j + 1) * NOPE
-            ]
+            )
+            pair = rope[:, j // 2 * NOPE : (j // 2 + 1) * NOPE]
+            pair = jnp.where(low, pair, 0.0) if j % 2 == 0 else jnp.where(low, 0.0, pair)
+            place = pl.ds(base + j * tokens, tokens)
+            absorbed[place, 0:LAT] = (product * scaling).astype(jnp.bfloat16)
+            absorbed[place, LAT:KEY] = pair.astype(jnp.bfloat16)
         return carry
 
     lax.fori_loop(0, HEADS // STACK, absorb, 0)
+
+    def scores(query, begin, blocks):
+        found = contract_last(query, keys[begin * rows : (begin + blocks) * rows, :])
+        found = found.reshape(STACK, tokens, blocks * rows)
+        bias = jnp.concatenate([bias_ref[:, 0:rows]] * blocks, axis=1)
+        return found + bias[None]
+
+    def flat(values):
+        return values.reshape(STACK * tokens, values.shape[2])
+
+    first[0].wait_recv()
+
+    def attend_near(group, carry):
+        place = pl.ds(pl.multiple_of(group * STACK * tokens, STACK * tokens), STACK * tokens)
+        query = absorbed[place, :]
+        far = scores(query, 0, 2)
+        near = contract_last(query, local_ref[...]).reshape(STACK, tokens, tokens)
+        near = near + bias_ref[:, rows:][None]
+        largest = jnp.maximum(
+            jnp.max(far, axis=2, keepdims=True), jnp.max(near, axis=2, keepdims=True)
+        )
+        far = jnp.exp2(far - largest)
+        near = jnp.exp2(near - largest)
+        total_max[place, :] = flat(largest)
+        total_sum[place, :] = flat(
+            jnp.sum(far, axis=2, keepdims=True) + jnp.sum(near, axis=2, keepdims=True)
+        )
+        total_out[place, :] = jnp.dot(
+            flat(far).astype(jnp.bfloat16),
+            keys[0 : 2 * rows, 0:LAT],
+            preferred_element_type=jnp.float32,
+        ) + jnp.dot(
+            flat(near).astype(jnp.bfloat16),
+            local_ref[:, 0:LAT],
+            preferred_element_type=jnp.float32,
+        )
+        return carry
+
+    lax.fori_loop(0, HEADS // STACK, attend_near, 0)
 
     second = []
     for k in range(1, half):
         first[k].wait_recv()
-        source = lax.rem(me + wide_count - 2 * k, wide_count)
         copy = pltpu.make_async_remote_copy(
-            src_ref=keys.at[slot(source)],
-            dst_ref=keys.at[slot(source)],
+            src_ref=keys.at[slot(2 * k)],
+            dst_ref=keys.at[slot(2 * k + 1)],
             send_sem=pass_sem.at[k - 1],
             recv_sem=land_sem.at[k - 1],
             device_id={"wide": sibling},
@@ -122,30 +167,24 @@
         )
         copy.start()
         second.append(copy)
-    first[0].wait_recv()
     for copy in second:
         copy.wait_recv()
 
     def attend(group, carry):
-        base = pl.multiple_of(group * STACK * tokens, STACK * tokens)
-        query = absorbed[pl.ds(base, STACK * tokens), :]
-        far = contract_last(query, keys[...]).reshape(STACK, tokens, far_rows)
-        near = contract_last(query, local_ref[...]).reshape(STACK, tokens, tokens)
-        far = far + bias_ref[:, 0:far_rows][None]
-        near = near + bias_ref[:, far_rows:][None]
-        largest = jnp.maximum(
-            jnp.max(far, axis=2, keepdims=True), jnp.max(near, axis=2, keepdims=True)
-        )
-        far = jnp.exp((far - largest) * scaling)
-        near = jnp.exp((near - largest) * scaling)
-        total = jnp.sum(far, axis=2, keepdims=True) + jnp.sum(near, axis=2, keepdims=True)
-        far16 = far.astype(jnp.bfloat16).reshape(STACK * tokens, far_rows)
-        near16 = near.astype(jnp.bfloat16).reshape(STACK * tokens, tokens)
-        mixed = jnp.dot(far16, keys[:, 0:LAT], preferred_element_type=jnp.float32)
-        mixed = mixed + jnp.dot(near16, local_ref[:, 0:LAT], preferred_element_type=jnp.float32)
-        mixed = (mixed / total.reshape(STACK * tokens, 1)).astype(jnp.bfloat16)
-        start = pl.multiple_of(group * STACK * NOPE, STACK * NOPE)
-        weights = w_ref[:, pl.ds(pl.multiple_of(2 * start, 2 * STACK * NOPE), 2 * STACK * NOPE)]
+        place = pl.ds(pl.multiple_of(group * STACK * tokens, STACK * tokens), STACK * tokens)
+        far = scores(absorbed[place, :], 2, wide_count - 2)
+        before = total_max[place, :].reshape(STACK, tokens, 1)
+        largest = jnp.maximum(jnp.max(far, axis=2, keepdims=True), before)
+        far = jnp.exp2(far - largest)
+        keep = flat(jnp.exp2(before - largest))
+        total = keep * total_sum[place, :] + flat(jnp.sum(far, axis=2, keepdims=True))
+        mixed = keep * total_out[place, :] + jnp.dot(
+            flat(far).astype(jnp.bfloat16),
+            keys[2 * rows :, 0:LAT],
+            preferred_element_type=jnp.float32,
+        )
+        mixed = (mixed / total).astype(jnp.bfloat16)
+        weights = group_weights(group)
         parts = []
         for j in range(STACK):
             parts.append(
@@ -155,6 +194,7 @@
                     preferred_element_type=jnp.float32,
                 ).astype(jnp.bfloat16)
             )
+        start = pl.multiple_of(group * STACK * NOPE, STACK * NOPE)
         out_ref[:, pl.ds(start, STACK * NOPE)] = jnp.concatenate(parts, axis=1)
         return carry
 
@@ -174,32 +214,33 @@
         prefix_rope[0].transpose(1, 0, 2).reshape(ROPE, rows),
     )
     local = joined_keys(suffix_latent, suffix_rope)
-    query_rope = queries[:, HEADS * NOPE :].reshape(token_count, HEADS, ROPE)
-    query_rope = jnp.pad(query_rope, ((0, 0), (0, 0), (0, NOPE - ROPE)))
-    query_rope = query_rope.reshape(token_count, HEADS * NOPE)
     positions = jnp.arange(token_count, dtype=jnp.int32)
     causal = (segment[:, None] == segment[None, :]) & (positions[None, :] <= positions[:, None])
-    key_owner = jnp.tile(jnp.repeat(jnp.arange(PREF, dtype=jnp.int32), block_rows), wide_count)
+    key_owner = jnp.repeat(jnp.arange(PREF, dtype=jnp.int32), block_rows)
     allowed = jnp.concatenate([prefix[:, None] == key_owner[None, :], causal], axis=1)
     bias = jnp.where(allowed, 0.0, -jnp.inf).astype(jnp.float32)
     vmem = pl.BlockSpec(memory_space=pltpu.VMEM)
+    stacked = HEADS * token_count
     return pl.pallas_call(
         functools.partial(attention_kernel, wide_count),
         out_shape=jax.ShapeDtypeStruct((token_count, HEADS * NOPE), jnp.bfloat16),
-        in_specs=[vmem] * 6,
+        in_specs=[vmem] * 5,
         out_specs=vmem,
         scratch_shapes=[
             pltpu.VMEM((wide_count * rows, KEY), jnp.bfloat16),
-            pltpu.VMEM((HEADS * token_count, KEY), jnp.bfloat16),
+            pltpu.VMEM((stacked, KEY), jnp.bfloat16),
+            pltpu.VMEM((stacked, LAT), jnp.float32),
+            pltpu.VMEM((stacked, 1), jnp.float32),
+            pltpu.VMEM((stacked, 1), jnp.float32),
             pltpu.SemaphoreType.DMA((half,)),
             pltpu.SemaphoreType.DMA((half,)),
             pltpu.SemaphoreType.DMA((half - 1,)),
             pltpu.SemaphoreType.DMA((half - 1,)),
         ],
         compiler_params=pltpu.CompilerParams(
-            collective_id=0, has_side_effects=True, vmem_limit_bytes=52 * 2**20
+            collective_id=0, has_side_effects=True, vmem_limit_bytes=56 * 2**20
         ),
-    )(queries[:, : HEADS * NOPE], query_rope, own, local, bias, w_ukv)
+    )(queries, own, local, bias, w_ukv)
 
 
 def expert_half(rows, gate_up_weights, down_weights):

time: 270 us -> 248 us (0.919)
  Pallas kernels: 49.4 us -> 36.4 us
  local copies, waits for them, and re-layouts: 18.2 us -> 9.73 us
    pallas_call x1, Pallas kernels: 49.4 us -> 36.4 us  [attention(): pl.pallas_call(functools.partial(attention_kernel, wide_count), out_shape...]
    slice x3 -> x1, local copies, waits for them, and re-layouts: 3 us -> 0.25 us  [the longest x1 1.67 us: attention(): query_rope = queries[:, HEADS * NOPE:].reshape(token_count, HEADS, ROPE)]
    unnamed x24 -> x21, local copies, waits for them, and re-layouts: 9.94 us -> 8.14 us
where the time goes in v2:
time: 248 us
  blocking collectives  81.2 us (33%)
  waiting for transfers between devices  80.3 us (32%)
  Pallas kernels  36.4 us (15%)
  matrix products  26.1 us (11%)
  other arithmetic  9.82 us (4%)
  local copies, waits for them, and re-layouts  9.73 us (4%)
  starting transfers between devices  3.94 us (2%)
    all_to_all x1, blocking collectives, exchange(): lax.all_to_all(rows.reshape(devices, share, lanes, 128), ('req', 'wide'),...  81.2 us
    all_to_all x1, waiting for transfers between devices, exchange(): lax.all_to_all(rows.reshape(devices, share, lanes, 128), ('req', 'wide'),...  74 us
    pallas_call x1, Pallas kernels, attention(): pl.pallas_call(functools.partial(attention_kernel, wide_count), out_shape...  36.4 us
    dot_general x2, matrix products, expert_half(): gate_up = jnp.dot(rows, gate_up_weights, preferred_element_type=jnp.float32)  10.5 us
    unnamed x21, local copies, waits for them, and re-layouts  8.14 us
    dot_general x2, matrix products, expert_half(): jnp.dot(activated, down_weights, preferred_element_type=jnp.float32)  6.28 us
    ppermute x1, waiting for transfers between devices, body(): other_rows = lax.ppermute(own_rows, 'wide', swap)  5.83 us
    dot_general x1, matrix products, body(): projected = jnp.dot(head_out, w_out, preferred_element_type=jnp.float32)  4.96 us
  transfers between devices with their start and end apart: 3, of which 3 were waited for; matrix products, arithmetic and copies ran while one was open for 2% of the time, Pallas kernels for 0%

profile of v2, /device:TPU:0, one launch (start us, length us, event | category | flops | bytes accessed | tf_op | source)
XLA Modules:
  0.0 247.8 jit_solution(3108191856028135583)
XLA Ops:
  0.0 0.0 copy-start
  0.0 0.9 copy.41
  0.9 0.1 eq.171
  1.1 0.1 eq.167
  1.2 1.7 reduce-window.19
  3.0 0.3 slice_reduce_fusion
  3.2 0.1 fusion.43
  3.3 0.1 reduce_sum.41
  3.5 0.1 copy.44
  3.5 0.7 multiply_add_fusion
  4.3 0.8 reduce-window.18
  5.1 0.1 convert_reduce_fusion
  5.2 0.1 fusion.41
  5.3 0.7 select_reduce_fusion
  6.0 0.9 copy.39
  6.9 0.8 copy.40
  7.7 0.1 broadcast_compare_fusion
  7.8 0.7 add_select_fusion.bias_ref
  8.5 1.8 pad_maximum_fusion.own_ref
  10.3 0.0 copy-start.3
  10.3 1.7 pad_maximum_fusion.1.local_ref
  12.0 36.4 %shard_map.145 = bf16[128,2048]{1,0:T(8,128)(2,1)} custom-call(bf16[128,3072]{1,0:T(8,128)(2,1)} %query_ref.1, bf16[256,640]{1,0:T(8,128)(2,1)} %pad_maximum_fusion.own_ref, bf16[128,640]{1,0:T(8,128)(2,1)} %pad_maximum_fusion.1.local_ref, f32[128,384]{1,0:T(8,128)} %add_select_fusion.bias_ref, bf16[512,4096]{1,0:T(8,128)(2,1)} %w_ref.1), custom_call_target="tpu_custom_call" | custom-call | tf_op jit(solution)/shard_map/pallas_call | solution.py:224
  48.4 0.0 copy-done.3
  48.4 0.0 copy-start.4
  48.4 5.0 %multiply_reduce_fusion = (f32[128]{0:T(128)S(1)}, f32[128,2048]{1,0:T(8,128)S(1)}) fusion(bf16[128,2048]{1,0:T(8,128)(2,1)} %shard_map.145, bf16[2048,2048]{1,0:T(8,128)(2,1)} %param.24, bf16[128,2048]{1,0:T(8,128)(2,1)S(1)} %copy-done.3), kind=kOutput, calls=%fused_computation.29 | convolution fusion | flops 1075314560 | bytes 10486272 | tf_op jit(solution)/shard_map/dot_general | solution.py:282
  53.4 0.0 copy-start.1
  53.4 0.0 copy-done.4
  53.5 1.0 copy-done.1
  54.4 1.1 fusion.14
  55.6 0.0 slice-start
  55.6 1.0 copy.46
  56.6 0.0 slice-start.1
  56.7 81.2 %all_to_all.10 = bf16[32,25,16,128]{3,2,1,0:T(8,128)(2,1)S(1)} all-to-all(bf16[32,25,16,128]{3,2,1,0:T(8,128)(2,1)S(1)} %bitcast.90), channel_id=1, replica_groups=mesh['req'=4,'wide'=8] {'req','wide'}, dimensions={0} | all-to-all | bytes 6553600 | tf_op jit(solution)/shard_map/all_to_all | solution.py:310
  137.9 1.5 copy.57
  139.4 0.1 collective-permute-start
  139.5 5.8 %collective-permute-done = bf16[800,2048]{1,0:T(8,128)(2,1)S(1)} collective-permute-done((bf16[800,2048]{1,0:T(8,128)(2,1)S(1)}, bf16[800,2048]{1,0:T(8,128)(2,1)S(1)}, u32[]{:S(2)}, u32[]{:S(2)}) %collective-permute-start) | collective-permute-done | bytes 3276832 | tf_op jit(solution)/shard_map/ppermute | solution.py:320
  145.3 0.0 slice-done
  145.3 0.0 slice-done.1
  145.3 5.2 %fusion = f32[800,1408]{1,0:T(8,128)S(1)} fusion(bf16[800,2048]{1,0:T(8,128)(2,1)S(1)} %collective-permute-done, bf16[1,2048,1408]{2,1,0:T(8,128)(2,1)S(1)} %bitcast.98), kind=kOutput, calls=%fused_computation.1 | convolution fusion | flops 4613734400 | bytes 13549568 | tf_op jit(solution)/shard_map/dot_general | solution.py:247
  150.6 0.0 copy-done
  150.6 3.1 %convolution_convert_fusion.1 = bf16[800,2048]{1,0:T(8,128)(2,1)S(1)} fusion(bf16[1,704,2048]{2,1,0:T(8,128)(2,1)S(1)} %copy-done, f32[800,1408]{1,0:T(8,128)S(1)} %fusion), kind=kOutput, calls=%fused_computation.6 | convolution fusion | flops 2311884800 | bytes 11075584 | tf_op jit(solution)/shard_map/dot_general | solution.py:252
  153.7 0.2 collective-permute-start.1
  153.9 5.2 %fusion.2 = f32[800,1408]{1,0:T(8,128)S(1)} fusion(bf16[1,2048,1408]{2,1,0:T(8,128)(2,1)S(1)} %bitcast.98, bf16[100,8,16,128]{3,2,1,0:T(8,128)(2,1)S(1)} %bitcast.89), kind=kOutput, calls=%fused_computation.3 | convolution fusion | flops 4613734400 | bytes 13549568 | tf_op jit(solution)/shard_map/dot_general | solution.py:247
  159.1 0.5 collective-permute-done.1
  159.6 3.2 %fusion.4 = bf16[100,8,16,128]{3,1,2,0:T(8,128)(2,1)S(1)} fusion(bf16[800,2048]{1,0:T(8,128)(2,1)S(1)} %collective-permute-done.1, bf16[1,704,2048]{2,1,0:T(8,128)(2,1)S(1)} %copy-done, f32[800,1408]{1,0:T(8,128)S(1)} %fusion.2), kind=kOutput, calls=%fused_computation.8 | convolution fusion | flops 2318438400 | bytes 14352384 | tf_op jit(solution)/shard_map/dot_general | solution.py:252
  162.8 2.8 %copy.48 = bf16[100,8,16,128]{3,2,1,0:T(8,128)(2,1)} copy(bf16[100,8,16,128]{3,1,2,0:T(8,128)(2,1)S(1)} %fusion.4) | data formatting | bytes 6553600
  165.6 0.0 copy-start.5
  165.6 3.7 %all-to-all-start.1 = ((bf16[32,25,16,128]{3,2,1,0:T(8,128)(2,1)}), bf16[32,25,16,128]{3,2,1,0:T(8,128)(2,1)}, u32[]{:S(2)}, u32[]{:S(2)}) async-start(bf16[32,25,16,128]{3,2,1,0:T(8,128)(2,1)} %bitcast.87), calls=%async_computation.1 | async-start | bytes 6553600 | tf_op jit(solution)/shard_map/all_to_all | solution.py:310
  169.2 0.0 copy-done.5
  169.3 0.3 subtract_convert_fusion
  169.6 74.0 %all-to-all-done.1 = bf16[32,25,16,128]{3,2,1,0:T(8,128)(2,1)} async-done(((bf16[32,25,16,128]{3,2,1,0:T(8,128)(2,1)}), bf16[32,25,16,128]{3,2,1,0:T(8,128)(2,1)}, u32[]{:S(2)}, u32[]{:S(2)}) %all-to-all-start.1) | async-done | bytes 3276832 | tf_op jit(solution)/shard_map/all_to_all | solution.py:310
  243.5 0.0 copy-start.2
  243.5 3.3 %fusion.5 = f32[256,2048]{1,0:T(8,128)S(1)} fusion(bf16[100,8,16,128]{3,2,1,0:T(8,128)(2,1)} %bitcast.39, bf16[800,128]{1,0:T(8,128)(2,1)S(1)} %get-tuple-element.5, bf16[800,128]{1,0:T(8,128)(2,1)S(1)} %get-tuple-element.6), kind=kOutput, calls=%fused_computation.9 | convolution fusion | flops 839680000 | bytes 5783552 | tf_op jit(solution)/shard_map/dot_general | solution.py:327
  246.8 0.0 copy-done.2
  246.8 1.0 fusion.22
  (8 shorter events, 0.1 us)
Async XLA Ops:
  0.0 150.6 %copy-start = (bf16[1,704,2048]{2,1,0:T(8,128)(2,1)S(1)}, bf16[1,704,2048]{2,1,0:T(8,128)(2,1)}, u32[]{:S(2)}) copy-start(bf16[1,704,2048]{2,1,0:T(8,128)(2,1)} %param.29) | copy-start | bytes 8650756
  10.3 38.1 %copy-start.3 = (bf16[128,2048]{1,0:T(8,128)(2,1)S(1)}, bf16[128,2048]{1,0:T(8,128)(2,1)}, u32[]{:S(2)}) copy-start(bf16[128,2048]{1,0:T(8,128)(2,1)} %param.18) | copy-start | bytes 1572868
  48.4 5.0 %copy-start.4 = (bf16[2048]{0:T(1024)(128)(2,1)S(1)}, bf16[2048]{0:T(1024)(128)(2,1)}, u32[]{:S(2)}) copy-start(bf16[2048]{0:T(1024)(128)(2,1)} %param.25) | copy-start | bytes 12292
  53.4 1.0 copy-start.1
  55.6 89.8 %slice-start = ((s8[5767168]{0:T(1024)(128)(4,1)}), s8[4194304]{0:T(1024)(128)(4,1)S(1)}, s32[]{:S(2)}) async-start(s8[5767168]{0:T(1024)(128)(4,1)} %bitcast.97), calls=%async_computation.2 | async-start | bytes 8388608
  56.6 88.7 %slice-start.1 = ((s8[5767168]{0:T(1024)(128)(4,1)}), s8[1572864]{0:T(1024)(128)(4,1)S(1)}, s32[]{:S(2)}) async-start(s8[5767168]{0:T(1024)(128)(4,1)} %bitcast.97), calls=%async_computation.3 | async-start | bytes 3145728
  139.4 5.9 %collective-permute-start = (bf16[800,2048]{1,0:T(8,128)(2,1)S(1)}, bf16[800,2048]{1,0:T(8,128)(2,1)S(1)}, u32[]{:S(2)}, u32[]{:S(2)}) collective-permute-start(bf16[800,2048]{1,0:T(8,128)(2,1)S(1)} %bitcast.91), channel_id=1, source_target_pairs={{0,1},{1,0},{2,3},{3,2},{4,5},{5,4},{6,7},{7,6},{8,9},{9,8},{10,11... | collective-permute-start | bytes 9830408 | tf_op jit(solution)/shard_map/ppermute | solution.py:320
  153.7 5.9 %collective-permute-start.1 = (bf16[800,2048]{1,0:T(8,128)(2,1)S(1)}, bf16[800,2048]{1,0:T(8,128)(2,1)S(1)}, u32[]{:S(2)}, u32[]{:S(2)}) collective-permute-start(bf16[800,2048]{1,0:T(8,128)(2,1)S(1)} %convolution_convert_fusion.1), channel_id=1, source_target_pairs={{0,1},{1,0},{2,3},{3,2},{4,5},{5,4},{6,7},{7,6},{8,9},{9,8},{10,11... | collective-permute-start | bytes 9830408 | tf_op jit(solution)/shard_map/ppermute | solution.py:323
  165.6 3.7 %copy-start.5 = (f32[128,6]{0,1:T(8,128)S(1)}, f32[128,6]{0,1:T(8,128)}, u32[]{:S(2)}) copy-start(f32[128,6]{0,1:T(8,128)} %param.27) | copy-start | bytes 9220
  165.6 78.0 %all-to-all-start.1 = ((bf16[32,25,16,128]{3,2,1,0:T(8,128)(2,1)}), bf16[32,25,16,128]{3,2,1,0:T(8,128)(2,1)}, u32[]{:S(2)}, u32[]{:S(2)}) async-start(bf16[32,25,16,128]{3,2,1,0:T(8,128)(2,1)} %bitcast.87), calls=%async_computation.1 | async-start | bytes 6553600 | tf_op jit(solution)/shard_map/all_to_all | solution.py:310
  243.5 3.3 %copy-start.2 = (f32[128,2048]{1,0:T(8,128)S(1)}, f32[128,2048]{1,0:T(8,128)}, u32[]{:S(2)}) copy-start(f32[128,2048]{1,0:T(8,128)} %copy-done.1) | copy-start | bytes 3145732

commit v3 on v2

--- a/solution.py
+++ b/solution.py
@@ -243,6 +243,244 @@
     )(queries, own, local, bias, w_ukv)
 
 
+def mesh_peers():
+    me_req, me_wide = lax.axis_index("req"), lax.axis_index("wide")
+    req_count, wide_count = lax.axis_size("req"), lax.axis_size("wide")
+    above = [lax.rem(me_req + k, req_count) for k in range(req_count)]
+    beside = [lax.rem(me_wide + j, wide_count) for j in range(wide_count)]
+    return above, beside
+
+
+def greet(above, beside):
+    barrier = pltpu.get_barrier_semaphore()
+    for peer in above[1:]:
+        pl.semaphore_signal(
+            barrier, inc=1, device_id={"req": peer}, device_id_type=pl.DeviceIdType.MESH
+        )
+    for peer in beside[1:]:
+        pl.semaphore_signal(
+            barrier, inc=1, device_id={"wide": peer}, device_id_type=pl.DeviceIdType.MESH
+        )
+    pl.semaphore_wait(barrier, len(above) + len(beside) - 2)
+
+
+def send(src, dst, send_sem, recv_sem, target):
+    copy = pltpu.make_async_remote_copy(
+        src_ref=src,
+        dst_ref=dst,
+        send_sem=send_sem,
+        recv_sem=recv_sem,
+        device_id=target,
+        device_id_type=pl.DeviceIdType.MESH,
+    )
+    copy.start()
+    return copy
+
+
+def dispatch_kernel(
+    share,
+    normed_ref,
+    select_ref,
+    out_ref,
+    tokens,
+    selects,
+    picked,
+    token_sems,
+    select_sems,
+    row_send,
+    row_recv,
+    own_sem,
+):
+    above, beside = mesh_peers()
+    greet(above, beside)
+    layer_rows = picked.shape[1]
+    layer = lambda r: pl.ds(pl.multiple_of(r * layer_rows, layer_rows), layer_rows)
+    piece = lambda w: pl.ds(pl.multiple_of(w * share, share), share)
+    sent, asked, moved, kept = [None], [None], [], []
+    for k in range(1, len(above)):
+        target = {"req": above[k]}
+        asked.append(
+            send(
+                select_ref.at[layer(above[k])],
+                selects.at[k - 1],
+                select_sems.at[0, k - 1],
+                select_sems.at[1, k - 1],
+                target,
+            )
+        )
+        sent.append(
+            send(
+                normed_ref,
+                tokens.at[k - 1],
+                token_sems.at[0, k - 1],
+                token_sems.at[1, k - 1],
+                target,
+            )
+        )
+    for k in range(len(above)):
+        if k == 0:
+            block, choice = normed_ref[...], select_ref[layer(above[0]), :]
+        else:
+            asked[k].wait_recv()
+            sent[k].wait_recv()
+            block, choice = tokens[k - 1], selects[k - 1]
+        picked[k] = jnp.dot(choice, block, preferred_element_type=jnp.float32).astype(jnp.bfloat16)
+        for j in range(1, len(beside)):
+            moved.append(
+                send(
+                    picked.at[k, piece(beside[j])],
+                    out_ref.at[k, j],
+                    row_send.at[k, j - 1],
+                    row_recv.at[k, j - 1],
+                    {"wide": beside[j]},
+                )
+            )
+        copy = pltpu.make_async_copy(
+            picked.at[k, piece(beside[0])], out_ref.at[k, 0], own_sem.at[k]
+        )
+        copy.start()
+        kept.append(copy)
+    for copy in moved:
+        copy.wait()
+    for copy in kept:
+        copy.wait()
+    for copy in asked[1:] + sent[1:]:
+        copy.wait_send()
+
+
+def combine_kernel(
+    share,
+    rows_ref,
+    gate_ref,
+    hidden_ref,
+    out_ref,
+    gates,
+    held,
+    partial,
+    arrived,
+    gate_sems,
+    row_send,
+    row_recv,
+    own_sem,
+    part_sems,
+):
+    above, beside = mesh_peers()
+    greet(above, beside)
+    layers, places = len(above), len(beside)
+    layer_rows = held.shape[1]
+    layer = lambda r: pl.ds(pl.multiple_of(r * layer_rows, layer_rows), layer_rows)
+    mine = pl.ds(pl.multiple_of(beside[0] * share, share), share)
+    order = list(range(1, layers)) + [0]
+    given = [None] + [
+        send(
+            gate_ref.at[layer(above[k])],
+            gates.at[k - 1],
+            gate_sems.at[0, k - 1],
+            gate_sems.at[1, k - 1],
+            {"req": above[k]},
+        )
+        for k in range(1, layers)
+    ]
+    moved, kept = {}, {}
+    for k in order:
+        for j in range(1, places):
+            moved[k, j] = send(
+                rows_ref.at[k, j],
+                held.at[k, mine],
+                row_send.at[k, j - 1],
+                row_recv.at[k, j - 1],
+                {"wide": beside[places - j]},
+            )
+        kept[k] = pltpu.make_async_copy(rows_ref.at[k, 0], held.at[k, mine], own_sem.at[k])
+        kept[k].start()
+    parts = []
+    total = None
+    for k in order:
+        for j in range(1, places):
+            moved[k, j].wait_recv()
+        kept[k].wait()
+        if k:
+            given[k].wait_recv()
+            weights = gates[k - 1]
+        else:
+            weights = gate_ref[layer(above[0]), :]
+        mixed = lax.dot_general(
+            weights, held[k], (((0,), (0,)), ((), ())), preferred_element_type=jnp.float32
+        )
+        if k:
+            partial[k - 1] = mixed.astype(jnp.bfloat16)
+            parts.append(
+                send(
+                    partial.at[k - 1],
+                    arrived.at[k - 1],
+                    part_sems.at[0, k - 1],
+                    part_sems.at[1, k - 1],
+                    {"req": above[layers - k]},
+                )
+            )
+        else:
+            total = mixed + hidden_ref[...].astype(jnp.float32)
+    for k, copy in enumerate(parts):
+        copy.wait_recv()
+        total = total + arrived[k].astype(jnp.float32)
+    out_ref[...] = total.astype(jnp.bfloat16)
+    for copy in given[1:] + list(moved.values()) + parts:
+        copy.wait_send()
+
+
+def dispatch(normed, select, share):
+    req_count, wide_count = lax.axis_size("req"), lax.axis_size("wide")
+    token_count = normed.shape[0]
+    vmem = pl.BlockSpec(memory_space=pltpu.VMEM)
+    dma = pltpu.SemaphoreType.DMA
+    return pl.pallas_call(
+        functools.partial(dispatch_kernel, share),
+        out_shape=jax.ShapeDtypeStruct((req_count, wide_count, share, D), jnp.bfloat16),
+        in_specs=[vmem, vmem],
+        out_specs=pl.BlockSpec(memory_space=pl.ANY),
+        scratch_shapes=[
+            pltpu.VMEM((req_count - 1, token_count, D), jnp.bfloat16),
+            pltpu.VMEM((req_count - 1, wide_count * share, token_count), jnp.bfloat16),
+            pltpu.VMEM((req_count, wide_count * share, D), jnp.bfloat16),
+            dma((2, req_count - 1)),
+            dma((2, req_count - 1)),
+            dma((req_count, wide_count - 1)),
+            dma((req_count, wide_count - 1)),
+            dma((req_count,)),
+        ],
+        compiler_params=pltpu.CompilerParams(
+            collective_id=1, has_side_effects=True, vmem_limit_bytes=48 * 2**20
+        ),
+    )(normed, select)
+
+
+def combine(rows, gates, hidden, share):
+    req_count, wide_count = lax.axis_size("req"), lax.axis_size("wide")
+    token_count = hidden.shape[0]
+    vmem = pl.BlockSpec(memory_space=pltpu.VMEM)
+    dma = pltpu.SemaphoreType.DMA
+    return pl.pallas_call(
+        functools.partial(combine_kernel, share),
+        out_shape=jax.ShapeDtypeStruct((token_count, D), jnp.bfloat16),
+        in_specs=[pl.BlockSpec(memory_space=pl.ANY), vmem, vmem],
+        out_specs=vmem,
+        scratch_shapes=[
+            pltpu.VMEM((req_count - 1, wide_count * share, token_count), jnp.bfloat16),
+            pltpu.VMEM((req_count, wide_count * share, D), jnp.bfloat16),
+            pltpu.VMEM((req_count - 1, token_count, D), jnp.bfloat16),
+            pltpu.VMEM((req_count - 1, token_count, D), jnp.bfloat16),
+            dma((2, req_count - 1)),
+            dma((req_count, wide_count - 1)),
+            dma((req_count, wide_count - 1)),
+            dma((req_count,)),
+            dma((2, req_count - 1)),
+        ],
+        compiler_params=pltpu.CompilerParams(
+            collective_id=2, has_side_effects=True, vmem_limit_bytes=48 * 2**20
+        ),
+    )(rows, gates, hidden)
+
+
 def expert_half(rows, gate_up_weights, down_weights):
     gate_up = jnp.dot(rows, gate_up_weights, preferred_element_type=jnp.float32)
     half_width = gate_up.shape[1] // 2
@@ -286,49 +524,27 @@
     normed = (hidden_f32 * inverse * norm_gain.astype(jnp.float32)[None, :]).astype(jnp.bfloat16)
 
     experts = devices // 2
-    share = (token_count * TOP // experts + 2) // 2
-    capacity = 2 * share
+    used = (token_count * TOP // experts + 2) // 2
+    share = (used + 15) // 16 * 16
     flat_ids = expert_ids.reshape(-1)
     one_hot = (flat_ids[:, None] == jnp.arange(experts, dtype=jnp.int32)[None, :]).astype(jnp.int32)
     slot_index = jnp.sum((jnp.cumsum(one_hot, axis=0) - 1) * one_hot, axis=1)
-    target = (flat_ids * capacity + slot_index).reshape(token_count, TOP)
-    slots = jnp.arange(experts * capacity, dtype=jnp.int32)
+    second = (slot_index >= used).astype(jnp.int32)
+    target = (2 * flat_ids + second) * share + slot_index - second * used
+    target = target.reshape(token_count, TOP)
+    slots = jnp.arange(devices * share, dtype=jnp.int32)
     placed = [slots[:, None] == target[None, :, k] for k in range(TOP)]
-    dispatch_rows = functools.reduce(jnp.logical_or, placed).astype(jnp.bfloat16)
-    combine_rows = sum(
-        jnp.where(placed[k], gate_values[None, :, k], 0.0) for k in range(TOP)
-    )
-    combine_high = combine_rows.astype(jnp.bfloat16)
-    combine_low = (combine_rows - combine_high.astype(jnp.float32)).astype(jnp.bfloat16)
-    outgoing = jnp.dot(dispatch_rows, normed, preferred_element_type=jnp.float32).astype(
-        jnp.bfloat16
-    )
-    lanes = D // 128
+    select = functools.reduce(jnp.logical_or, placed).astype(jnp.bfloat16)
+    gates = sum(jnp.where(placed[k], gate_values[None, :, k], 0.0) for k in range(TOP))
+    gates = gates.astype(jnp.bfloat16)
     swap = [(i, i ^ 1) for i in range(wide_count)]
-
-    def exchange(rows):
-        moved = lax.all_to_all(
-            rows.reshape(devices, share, lanes, 128),
-            ("req", "wide"),
-            split_axis=0,
-            concat_axis=0,
-            tiled=True,
-        )
-        return moved.reshape(devices * share, D)
-
-    own_rows = exchange(outgoing)
+    own_rows = dispatch(normed, select, share).reshape(devices * share, D)
     other_rows = lax.ppermute(own_rows, "wide", swap)
-    own_half = expert_half(own_rows, expert_gate_up[0], expert_down[0])
     other_half = expert_half(other_rows, expert_gate_up[0], expert_down[0])
     arrived = lax.ppermute(other_half, "wide", swap)
+    own_half = expert_half(own_rows, expert_gate_up[0], expert_down[0])
     summed = (own_half.astype(jnp.float32) + arrived.astype(jnp.float32)).astype(jnp.bfloat16)
-    returned = exchange(summed)
-    both = jnp.concatenate([combine_high, combine_low], axis=1)
-    mixture = lax.dot_general(
-        both, returned, (((0,), (0,)), ((), ())), preferred_element_type=jnp.float32
-    )
-    mixture = mixture[:token_count] + mixture[token_count:]
-    return (hidden_f32 + mixture).astype(jnp.bfloat16)
+    return combine(summed.reshape(req_count, wide_count, share, D), gates, hidden, share)
 
 
 def solution(mesh):

time: 248 us -> 228 us (0.919)
  Pallas kernels: 36.4 us -> 179 us
  blocking collectives: 81.2 us -> 0 us
  waiting for transfers between devices: 80.3 us -> 6.79 us
  local copies, waits for them, and re-layouts: 9.73 us -> 4.19 us
    pallas_call x0 -> x2, Pallas kernels: none -> 142 us  [the longest x1 74.6 us: combine(): pl.pallas_call(functools.partial(combine_kernel, share), out_shape=jax.Sh...]
    all_to_all x1 -> x0, blocking collectives: 81.2 us -> none  [exchange(): lax.all_to_all(rows.reshape(devices, share, lanes, 128), ('req', 'wide'),...]
    all_to_all x1 -> x0, waiting for transfers between devices: 74 us -> none  [exchange(): lax.all_to_all(rows.reshape(devices, share, lanes, 128), ('req', 'wide'),...]
    unnamed x21 -> x15, local copies, waits for them, and re-layouts: 8.14 us -> 2.61 us
    dot_general x2 -> x0, matrix products: 4.43 us -> none  [the longest x1 3.28 us: body(): lax.dot_general(both, returned, (((0,), (0,)), ((), ())), preferred_eleme...]
    all_to_all x1 -> x0, starting transfers between devices: 3.67 us -> none  [exchange(): lax.all_to_all(rows.reshape(devices, share, lanes, 128), ('req', 'wide'),...]
    dot_general x2, matrix products: 10.5 us -> 13.3 us  [expert_half(): gate_up = jnp.dot(rows, gate_up_weights, preferred_element_type=jnp.float32)]
  transfers between devices with their start and end apart: 3 -> 2, of which waited for: 3 -> 1; matrix products, arithmetic and copies ran while one was open for 2% -> 3% of each run, Pallas kernels for 0% -> 0%
where the time goes in v3:
time: 228 us; the launch traced here: 227 us
  Pallas kernels  179 us (79%)
  matrix products  26.2 us (11%)
  other arithmetic  9.38 us (4%)
  waiting for transfers between devices  6.79 us (3%)
  local copies, waits for them, and re-layouts  4.19 us (2%)
    pallas_call x1, Pallas kernels, combine(): pl.pallas_call(functools.partial(combine_kernel, share), out_shape=jax.Sh...  74.6 us
    pallas_call x1, Pallas kernels, dispatch(): pl.pallas_call(functools.partial(dispatch_kernel, share), out_shape=jax.S...  67.8 us
    pallas_call x1, Pallas kernels, attention(): pl.pallas_call(functools.partial(attention_kernel, wide_count), out_shape...  36.5 us
    dot_general x2, matrix products, expert_half(): gate_up = jnp.dot(rows, gate_up_weights, preferred_element_type=jnp.float32)  13.3 us
    dot_general x2, matrix products, expert_half(): jnp.dot(activated, down_weights, preferred_element_type=jnp.float32)  7.81 us
    ppermute x1, waiting for transfers between devices, body(): other_rows = lax.ppermute(own_rows, 'wide', swap)  6.79 us
    dot_general x1, matrix products, body(): projected = jnp.dot(head_out, w_out, preferred_element_type=jnp.float32)  5.11 us
  transfers between devices with their start and end apart: 2, of which 1 were waited for; matrix products, arithmetic and copies ran while one was open for 3% of the time, Pallas kernels for 0%

profile of v3, /device:TPU:0, one launch (start us, length us, event | category | flops | bytes accessed | tf_op | source)
XLA Modules:
  0.0 227.4 jit_solution(3368863580846315073)
XLA Ops:
  0.0 0.0 copy-start
  0.0 0.0 copy-start.1
  0.0 0.9 copy.47
  1.0 0.1 eq.171
  1.1 0.1 eq.167
  1.3 1.7 reduce-window.19
  3.0 0.3 slice_reduce_fusion
  3.3 0.1 fusion.24
  3.4 0.1 reduce_sum.42
  3.5 0.1 copy.50
  3.6 0.7 select_subtract_fusion
  4.3 0.8 reduce-window.18
  5.1 0.1 convert_reduce_fusion
  5.2 0.1 fusion.22
  5.3 0.7 select_reduce_fusion
  6.0 0.9 copy.45
  6.9 0.8 copy.46
  7.7 0.1 broadcast_compare_fusion
  7.8 0.7 add_select_fusion.bias_ref
  8.5 1.8 pad_maximum_fusion.own_ref
  10.3 1.6 pad_maximum_fusion.1.local_ref
  11.9 0.0 slice-start
  11.9 36.5 %shard_map.145 = bf16[128,2048]{1,0:T(8,128)(2,1)} custom-call(bf16[128,3072]{1,0:T(8,128)(2,1)} %query_ref.1, bf16[256,640]{1,0:T(8,128)(2,1)} %pad_maximum_fusion.own_ref, bf16[128,640]{1,0:T(8,128)(2,1)} %pad_maximum_fusion.1.local_ref, f32[128,384]{1,0:T(8,128)} %add_select_fusion.bias_ref, bf16[512,4096]{1,0:T(8,128)(2,1)} %w_ref.1), custom_call_target="tpu_custom_call" | custom-call | tf_op jit(solution)/shard_map/pallas_call | solution.py:224
  48.5 0.0 copy-done.1
  48.5 0.0 copy-start.2
  48.5 0.0 slice-start.1
  48.5 5.1 %fusion.13 = (f32[128]{0:T(128)S(1)}, bf16[128,2048]{1,0:T(8,128)(2,1)S(1)}) fusion(bf16[128,2048]{1,0:T(8,128)(2,1)} %shard_map.145, bf16[2048,2048]{1,0:T(8,128)(2,1)} %param.24, bf16[128,2048]{1,0:T(8,128)(2,1)S(1)} %copy-done.1), kind=kOutput, calls=%fused_computation.18 | convolution fusion | flops 1075314560 | bytes 9961984 | tf_op jit(solution)/shard_map/dot_general | solution.py:520
  53.6 0.0 copy-done.2
  53.7 0.2 fusion.15.normed_ref
  53.9 0.3 fusion.21.select_ref
  54.2 67.8 %shard_map.146 = bf16[4,8,32,2048]{3,2,1,0:T(8,128)(2,1)S(1)} custom-call(bf16[128,2048]{1,0:T(8,128)(2,1)S(1)} %fusion.15.normed_ref, bf16[1024,128]{1,0:T(8,128)(2,1)S(1)} %fusion.21.select_ref), custom_call_target="tpu_custom_call" | custom-call | tf_op jit(solution)/shard_map/pallas_call | solution.py:436
  122.0 1.3 collective-permute-start
  123.3 6.8 %collective-permute-done = bf16[1024,2048]{1,0:T(8,128)(2,1)S(1)} collective-permute-done((bf16[1024,2048]{1,0:T(8,128)(2,1)S(1)}, bf16[1024,2048]{1,0:T(8,128)(2,1)S(1)}, u32[]{:S(2)}, u32[]{:S(2)}) %collective-permute-start) | collective-permute-done | bytes 4194336 | tf_op jit(solution)/shard_map/ppermute | solution.py:542
  130.1 0.0 slice-done
  130.1 0.0 slice-done.1
  130.1 6.6 %fusion = f32[1024,1408]{1,0:T(8,128)S(1)} fusion(bf16[1024,2048]{1,0:T(8,128)(2,1)S(1)} %collective-permute-done, bf16[1,2048,1408]{2,1,0:T(8,128)(2,1)S(1)} %bitcast.78), kind=kOutput, calls=%fused_computation.1 | convolution fusion | flops 5905580032 | bytes 15728640 | tf_op jit(solution)/shard_map/dot_general | solution.py:485
  136.8 0.0 copy-done
  136.8 0.0 copy-start.3
  136.8 3.9 %convolution_convert_fusion = bf16[1024,2048]{1,0:T(8,128)(2,1)S(1)} fusion(bf16[1,704,2048]{2,1,0:T(8,128)(2,1)S(1)} %copy-done, f32[1024,1408]{1,0:T(8,128)S(1)} %fusion), kind=kOutput, calls=%fused_computation.5 | convolution fusion | flops 2959212544 | bytes 13369344 | tf_op jit(solution)/shard_map/dot_general | solution.py:490
  140.7 0.4 collective-permute-start.1
  141.1 0.0 copy-done.3
  141.1 0.3 add_convert_fusion.1.gate_ref
  141.5 6.6 %fusion.2 = f32[1024,1408]{1,0:T(8,128)S(1)} fusion(bf16[1024,2048]{1,0:T(8,128)(2,1)S(1)} %bitcast.70, bf16[1,2048,1408]{2,1,0:T(8,128)(2,1)S(1)} %bitcast.78), kind=kOutput, calls=%fused_computation.3 | convolution fusion | flops 5905580032 | bytes 15728640 | tf_op jit(solution)/shard_map/dot_general | solution.py:485
  148.1 0.0 collective-permute-done.1
  148.1 3.9 %add_convert_fusion = bf16[1024,2048]{1,0:T(8,128)(2,1)S(1)} fusion(bf16[1024,2048]{1,0:T(8,128)(2,1)S(1)} %collective-permute-done.1, bf16[1,704,2048]{2,1,0:T(8,128)(2,1)S(1)} %copy-done, f32[1024,1408]{1,0:T(8,128)S(1)} %fusion.2), kind=kOutput, calls=%fused_computation | convolution fusion | flops 2967601152 | bytes 17563648 | tf_op jit(solution)/shard_map/dot_general | solution.py:490
  152.0 74.6 %shard_map.147 = bf16[128,2048]{1,0:T(8,128)(2,1)S(1)} custom-call(bf16[4,8,32,2048]{3,2,1,0:T(8,128)(2,1)S(1)} %bitcast.71, bf16[1024,128]{1,0:T(8,128)(2,1)S(1)} %add_convert_fusion.1.gate_ref, bf16[128,2048]{1,0:T(8,128)(2,1)S(1)} %get-tuple-element.18.hidden_ref), custom_call_target="tpu_custom_call" | custom-call | tf_op jit(solution)/shard_map/pallas_call | solution.py:462
  226.6 0.8 copy.55
  (8 shorter events, 0.1 us)
Async XLA Ops:
  0.0 136.8 %copy-start = (bf16[1,704,2048]{2,1,0:T(8,128)(2,1)S(1)}, bf16[1,704,2048]{2,1,0:T(8,128)(2,1)}, u32[]{:S(2)}) copy-start(bf16[1,704,2048]{2,1,0:T(8,128)(2,1)} %param.29) | copy-start | bytes 8650756
  0.0 48.5 %copy-start.1 = (bf16[128,2048]{1,0:T(8,128)(2,1)S(1)}, bf16[128,2048]{1,0:T(8,128)(2,1)}, u32[]{:S(2)}) copy-start(bf16[128,2048]{1,0:T(8,128)(2,1)} %param.18) | copy-start | bytes 1572868
  11.9 118.2 %slice-start = ((s8[5767168]{0:T(1024)(128)(4,1)}), s8[1572864]{0:T(1024)(128)(4,1)S(1)}, s32[]{:S(2)}) async-start(s8[5767168]{0:T(1024)(128)(4,1)} %bitcast.77), calls=%async_computation | async-start | bytes 3145728
  48.5 5.2 %copy-start.2 = (bf16[2048]{0:T(1024)(128)(2,1)S(1)}, bf16[2048]{0:T(1024)(128)(2,1)}, u32[]{:S(2)}) copy-start(bf16[2048]{0:T(1024)(128)(2,1)} %param.25) | copy-start | bytes 12292
  48.5 81.6 %slice-start.1 = ((s8[5767168]{0:T(1024)(128)(4,1)}), s8[4194304]{0:T(1024)(128)(4,1)S(1)}, s32[]{:S(2)}) async-start(s8[5767168]{0:T(1024)(128)(4,1)} %bitcast.77), calls=%async_computation.1 | async-start | bytes 8388608
  122.0 8.1 %collective-permute-start = (bf16[1024,2048]{1,0:T(8,128)(2,1)S(1)}, bf16[1024,2048]{1,0:T(8,128)(2,1)S(1)}, u32[]{:S(2)}, u32[]{:S(2)}) collective-permute-start(bf16[1024,2048]{1,0:T(8,128)(2,1)S(1)} %bitcast.69), channel_id=1, source_target_pairs={{0,1},{1,0},{2,3},{3,2},{4,5},{5,4},{6,7},{7,6},{8,9},{9,8},{10,11... | collective-permute-start | bytes 12582920 | tf_op jit(solution)/shard_map/ppermute | solution.py:542
  136.8 4.4 %copy-start.3 = (f32[128,6]{0,1:T(8,128)S(1)}, f32[128,6]{0,1:T(8,128)}, u32[]{:S(2)}) copy-start(f32[128,6]{0,1:T(8,128)} %param.27) | copy-start | bytes 9220
  140.7 7.4 %collective-permute-start.1 = (bf16[1024,2048]{1,0:T(8,128)(2,1)S(1)}, bf16[1024,2048]{1,0:T(8,128)(2,1)S(1)}, u32[]{:S(2)}, u32[]{:S(2)}) collective-permute-start(bf16[1024,2048]{1,0:T(8,128)(2,1)S(1)} %convolution_convert_fusion), channel_id=1, source_target_pairs={{0,1},{1,0},{2,3},{3,2},{4,5},{5,4},{6,7},{7,6},{8,9},{9,8},{10,11... | collective-permute-start | bytes 12582920 | tf_op jit(solution)/shard_map/ppermute | solution.py:544
